TPU v7x, 32 devices: a whole 2x2x4 slice. The times are simulated.
32 devices in a mesh: grp: 2 (over y), ep: 4 (over z), pp: 4 (over x, core).
Axes of the slice: x: 2, y: 2, z: 4, core: 2. Of those that a mesh axis runs over, the one named last changes fastest.
Arguments:
- hidden: bfloat16 [4, 256, 3584], P('pp', ('grp', 'ep')), parts along dimension 1, may hold values from -6 to 6
- norm_gain: bfloat16 [4, 3584], P('pp'), may hold values from 0.25 to 1.75
- expert_ids: int32 [4, 256, 2], P('pp', ('grp', 'ep')), parts along dimension 1, may hold values from 0 to 3, all different within a row; in each aligned block of 32 rows (0 to 31, 32 to 63, ..., all dimensions but the last counted through in order) at most 24 rows name the same one
- gate_weights: float32 [4, 256, 2], P('pp', ('grp', 'ep')), parts along dimension 1, may hold values from 0.1 to 0.6
- expert_gate_up: bfloat16 [4, 4, 3584, 2048], P('pp', 'ep'), may hold values from -0.09375 to 0.09375
- expert_down: bfloat16 [4, 4, 1024, 3584], P('pp', 'ep'), may hold values from -0.1875 to 0.1875
- partner: int32 [8, 16], P(('grp', 'ep')), parts along dimension 0, may hold values from 0 to 15, each once within a row
Outputs:
- passed: bfloat16 [4, 256, 3584], P('pp', ('grp', 'ep')), parts along dimension 1
There are 2 independent parts, one for each index of `grp`. A program takes and returns all parts, laid end to end along the dimension named above; an argument that names none is the same for every part. Nothing has to cross between parts.
Inputs may be any that keep to these rules, and one draw needn't show every extreme that they name: `expert_ids`: each row names 2 different experts. Within the rows of one device (aligned blocks of 32 rows) no expert is named by more than 24 rows, and some block reaches 24. `partner`: the entries of each device's block are a permutation of the indices of its weak rows.
All inputs are finite; a program needn't handle non-finite values.
Results may differ from a plain program's by a relative error of at most 0.0034.
Values may be sent and summed in bfloat16 or wider, within the bound.
No kernel may reach another device: no remote copies, remote signals or barrier semaphores. Data moves between devices by JAX's collectives and lax.ppermute only.
A program may use at most 64 MiB of HBM per device.

v0:
```python
import jax
import jax.numpy as jnp
from jax import lax
from jax.sharding import PartitionSpec as P

EXPERTS = 4
TOP = 2
CAP = 24


guidance_scale = 2.5
epsilon = 1e-06


def from_behind(shard, axis, by):
    devices = lax.axis_size(axis)
    return lax.ppermute(shard, axis, [(i, (i + by) % devices) for i in range(devices)])


def slot_positions(membership):
    per_row = jnp.sum(membership, axis=-2)
    earlier = jnp.cumsum(per_row, axis=-2) - per_row
    return jnp.sum(membership * earlier[..., None, :], axis=-1)


def slot_matrix(membership, positions, capacity):
    slot_values = jnp.arange(capacity, dtype=jnp.float32)
    matches = (positions[..., None] == slot_values).astype(jnp.float32)
    return jnp.einsum("...rke,...rkc->...ecr", membership, matches)


def run_experts(arrived, gate_up, down_matrix):
    shard_width = down_matrix.shape[0]
    projected = jnp.einsum("scd,df->scf", arrived, gate_up, preferred_element_type=jnp.float32)
    active = (jax.nn.silu(projected[..., :shard_width]) * projected[..., shard_width:]).astype(
        jnp.bfloat16
    )
    return jnp.einsum(
        "scf,fd->scd", active, down_matrix, preferred_element_type=jnp.float32
    ).astype(jnp.bfloat16)


def send_back(results):
    return lax.all_to_all(results, "ep", split_axis=0, concat_axis=0, tiled=True)


def shards(hidden, norm_gain, expert_ids, gate_weights, expert_gate_up, expert_down, partner):
    section_rows = hidden[0]
    widened = section_rows.astype(jnp.float32)
    factor = lax.rsqrt(jnp.mean(widened * widened, axis=-1, keepdims=True) + epsilon)
    normed = (widened * factor * norm_gain[0].astype(jnp.float32)).astype(jnp.bfloat16)
    gate_up = expert_gate_up[0, 0]
    down_matrix = expert_down[0, 0]
    devices = lax.axis_size("ep")
    shards_each = devices // EXPERTS
    row_count = section_rows.shape[0]
    routed = expert_ids[0]
    membership = (routed[:, :, None] == jnp.arange(EXPERTS, dtype=jnp.int32)).astype(jnp.float32)
    positions = slot_positions(membership)
    gathered_rows, gathered_ids = (
        lax.all_gather(normed, "ep", axis=0, tiled=True),
        lax.all_gather(routed.astype(jnp.bfloat16), "ep", axis=0, tiled=True),
    )
    own_expert = lax.axis_index("ep") // shards_each
    source_ids = gathered_ids.astype(jnp.int32).reshape(devices, row_count, TOP)
    own_member = (source_ids == own_expert).astype(jnp.float32)[..., None]
    chosen = slot_matrix(own_member, slot_positions(own_member), CAP)[:, 0]
    arrived = jnp.einsum(
        "scr,srd->scd",
        chosen.astype(jnp.bfloat16),
        gathered_rows.reshape(devices, row_count, -1),
        preferred_element_type=jnp.float32,
    ).astype(jnp.bfloat16)
    returned = send_back(run_experts(arrived, gate_up, down_matrix))
    combined = jnp.sum(
        returned.reshape(EXPERTS, shards_each, CAP, -1).astype(jnp.float32), axis=1
    ).reshape(EXPERTS * CAP, -1)
    slot_index = routed * CAP + positions.astype(jnp.int32)
    picked = jnp.take(combined, slot_index, axis=0)
    mixture = jnp.sum(gate_weights[0][..., None] * picked, axis=1)
    layer_out = widened + mixture
    middle = row_count // 2
    weak_rows = layer_out[middle:]
    paired = jnp.take(weak_rows, partner[0], axis=0)
    guided = paired + guidance_scale * (layer_out[:middle] - paired)
    final = jnp.concatenate([guided, weak_rows], axis=0)
    is_last = lax.axis_index("pp") == lax.axis_size("pp") - 1
    section_out = jnp.where(is_last, final, layer_out).astype(jnp.bfloat16)
    moved = from_behind(section_out, "pp", 1)
    return moved[None]


def solution(mesh):
    return jax.shard_map(
        shards,
        mesh=mesh,
        in_specs=(
            P("pp", ("grp", "ep"), None),
            P("pp", None),
            P("pp", ("grp", "ep"), None),
            P("pp", ("grp", "ep"), None),
            P("pp", "ep", None, None),
            P("pp", "ep", None, None),
            P(("grp", "ep"), None),
        ),
        out_specs=P("pp", ("grp", "ep"), None),
        check_vma=False,
    )
```

profile of v0, /device:TPU:0, one launch (start us, length us, event | category | flops | bytes accessed | tf_op | source)
XLA Modules:
  0.0 75.8 jit_solution(2083324757955526442)
XLA Ops:
  0.0 0.7 convert_bitcast_fusion
  0.7 12.5 %all-gather = bf16[4,32,2]{1,2,0:T(2,128)(2,1)S(1)} all-gather(bf16[1,32,2]{1,2,0:T(2,128)(2,1)S(1)} %convert_bitcast_fusion), channel_id=1, replica_groups=mesh['grp'=2,'ep'=4,'pp'=4] {'ep'}, dimensions={0}, use_global_device_ids=true | all-gather | bytes 640 | tf_op jit(solution)/shard_map/all_gather | solution.py:62
  13.3 0.2 reduce_window_sum.26
  13.5 0.1 copy.28
  13.6 0.1 copy.35
  13.7 0.4 fusion.16
  14.1 0.1 copy.34
  14.2 0.8 convert_reduce_fusion
  14.9 1.1 %fusion.7 = f32[32]{0:T(128)S(1)} fusion(bf16[1,32,3584]{2,1,0:T(8,128)(2,1)} %param.7), kind=kLoop, calls=%fused_computation.13 | loop fusion | flops 344032 | bytes 229504 | tf_op jit(solution)/shard_map/reduce_sum | solution.py:50
  16.0 1.1 %fusion.9 = bf16[32,3584]{1,0:T(8,128)(2,1)S(1)} fusion(bf16[1,32,3584]{2,1,0:T(8,128)(2,1)} %param.7, f32[3584]{0:T(1024)S(1)} %convert_reduce_fusion, f32[32]{0:T(128)S(1)} %add_rsqrt_fusion), kind=kLoop, calls=%fused_computation.15 | loop fusion | flops 458752 | bytes 473216 | tf_op jit(solution)/shard_map/convert_element_type | solution.py:51
  17.1 17.9 %all_gather.7 = bf16[128,3584]{1,0:T(8,128)(2,1)S(1)} all-gather(bf16[32,3584]{1,0:T(8,128)(2,1)S(1)} %fusion.9), channel_id=1, replica_groups=mesh['grp'=2,'ep'=4,'pp'=4] {'ep'}, dimensions={0}, use_global_device_ids=true | all-gather | bytes 1146880 | tf_op jit(solution)/shard_map/all_gather | solution.py:61
  35.0 6.7 %fusion = f32[4,24,2048]{2,1,0:T(8,128)S(1)} fusion(bf16[1,1,3584,2048]{3,2,1,0:T(8,128)(2,1)} %param.11, bf16[4,32,3584]{2,1,0:T(8,128)(2,1)S(1)} %bitcast.51, bf16[4,32,24]{1,2,0:T(8,128)(2,1)S(1)} %copy.34), kind=kOutput, calls=%fused_computation.2 | convolution fusion | flops 1431650304 | bytes 16390144 | tf_op jit(solution)/shard_map/scd,df->scf/dot_general | solution.py:34
  41.7 5.3 %fusion.4 = bf16[4,24,3584]{2,1,0:T(8,128)(2,1)} fusion(bf16[1,1,1024,3584]{3,2,1,0:T(8,128)(2,1)} %param.12, f32[4,24,2048]{2,1,0:T(8,128)S(1)} %fusion), kind=kOutput, calls=%fused_computation.6 | convolution fusion | flops 705576960 | bytes 8814592 | tf_op jit(solution)/shard_map/scf,fd->scd/dot_general | solution.py:38
  47.0 4.2 %all-to-all-start = ((bf16[4,24,3584]{2,1,0:T(8,128)(2,1)}), bf16[4,24,3584]{2,1,0:T(8,128)(2,1)S(1)}, u32[]{:S(2)}, u32[]{:S(2)}) async-start(bf16[4,24,3584]{2,1,0:T(8,128)(2,1)} %fusion.4), calls=%async_computation | async-start | bytes 1376256 | tf_op jit(solution)/shard_map/all_to_all | solution.py:44
  51.3 0.1 copy.24
  51.3 0.1 reduce_window_sum.24
  51.4 0.1 copy.26
  51.5 0.1 copy.29
  51.6 0.1 reshape.156
  51.7 0.1 copy.27
  51.8 0.1 copy.23
  52.0 13.7 %all-to-all-done = bf16[4,24,3584]{2,1,0:T(8,128)(2,1)S(1)} async-done(((bf16[4,24,3584]{2,1,0:T(8,128)(2,1)}), bf16[4,24,3584]{2,1,0:T(8,128)(2,1)S(1)}, u32[]{:S(2)}, u32[]{:S(2)}) %all-to-all-start) | async-done | bytes 688160 | tf_op jit(solution)/shard_map/all_to_all | solution.py:44
  65.7 0.2 bitcast_convert_fusion
  65.8 0.9 %gather_fusion = f32[64,3584]{1,0:T(8,128)S(1)} fusion(f32[96,3584]{1,0:T(8,128)S(1)} %bitcast_convert_fusion, s32[1024]{0:T(1024)S(1)} %pad_clamp_fusion.1), kind=kCustom, calls=%fused_computation | custom fusion | bytes 1835264 | tf_op jit(solution)/shard_map/jit(_take)/gather | solution.py:79
  66.7 0.5 reshape.155
  67.3 1.4 %multiply_reduce_fusion = f32[32,3584]{1,0:T(8,128)S(1)} fusion(f32[32,2,3584]{2,1,0:T(2,128)S(1)} %reshape.155, pred[32,2]{1,0:T(8,128)(4,1)S(1)} %copy.27, f32[32,2]{1,0:T(8,128)S(1)} %copy.23), kind=kLoop, calls=%fused_computation.8 | loop fusion | flops 573440 | bytes 1376576 | tf_op jit(solution)/shard_map/reduce_sum | solution.py:80
  68.8 0.6 gather_fusion.1
  69.5 0.1 fusion.13
  69.6 0.1 fusion.10
  69.6 0.1 collective-permute-start
  69.7 5.4 %collective-permute-done = bf16[32,3584]{1,0:T(8,128)(2,1)S(1)} collective-permute-done((bf16[32,3584]{1,0:T(8,128)(2,1)S(1)}, bf16[32,3584]{1,0:T(8,128)(2,1)S(1)}, u32[]{:S(2)}, u32[]{:S(2)}) %collective-permute-start) | collective-permute-done | bytes 229408 | tf_op jit(solution)/shard_map/ppermute | solution.py:17
  75.1 0.7 copy.38
  (24 shorter events, 0.2 us)
Async XLA Ops:
  41.7 9.5 %copy-start.1 = (s32[1,32,2]{1,2,0:T(2,128)S(1)}, s32[1,32,2]{1,2,0:T(2,128)}, u32[]{:S(2)}) copy-start(s32[1,32,2]{1,2,0:T(2,128)} %param.9) | copy-start | bytes 772
  41.7 10.1 %copy-start.2 = (f32[1,32,2]{1,2,0:T(2,128)S(1)}, f32[1,32,2]{1,2,0:T(2,128)}, u32[]{:S(2)}) copy-start(f32[1,32,2]{1,2,0:T(2,128)} %param.10) | copy-start | bytes 772
  41.7 10.2 %copy-start.3 = (s32[1,16]{1,0:T(1,128)S(1)}, s32[1,16]{1,0:T(1,128)}, u32[]{:S(2)}) copy-start(s32[1,16]{1,0:T(1,128)} %param.13) | copy-start | bytes 196
  47.0 21.7 %copy-start = (bf16[1,32,3584]{2,1,0:T(8,128)(2,1)S(1)}, bf16[1,32,3584]{2,1,0:T(8,128)(2,1)}, u32[]{:S(2)}) copy-start(bf16[1,32,3584]{2,1,0:T(8,128)(2,1)} %param.7) | copy-start | bytes 688132
  47.0 18.6 %all-to-all-start = ((bf16[4,24,3584]{2,1,0:T(8,128)(2,1)}), bf16[4,24,3584]{2,1,0:T(8,128)(2,1)S(1)}, u32[]{:S(2)}, u32[]{:S(2)}) async-start(bf16[4,24,3584]{2,1,0:T(8,128)(2,1)} %fusion.4), calls=%async_computation | async-start | bytes 1376256 | tf_op jit(solution)/shard_map/all_to_all | solution.py:44
  69.6 5.5 %collective-permute-start = (bf16[32,3584]{1,0:T(8,128)(2,1)S(1)}, bf16[32,3584]{1,0:T(8,128)(2,1)S(1)}, u32[]{:S(2)}, u32[]{:S(2)}) collective-permute-start(bf16[32,3584]{1,0:T(8,128)(2,1)S(1)} %fusion.10), channel_id=1, source_target_pairs={{0,1},{1,2},{2,3},{3,0},{4,5},{5,6},{6,7},{7,4},{8,9},{9,10},{10,1... | collective-permute-start | bytes 688136 | tf_op jit(solution)/shard_map/ppermute | solution.py:17
where the time goes:
time: 76.2 us; the launch traced here: 75.8 us
  blocking collectives  30.4 us (40%)
  waiting for transfers between devices  19.1 us (25%)
  matrix products  12 us (16%)
  other arithmetic  6.17 us (8%)
  starting transfers between devices  4.25 us (6%)
  local copies, waits for them, and re-layouts  3.64 us (5%)
    all_gather x1, blocking collectives, shards(): lax.all_gather(normed, 'ep', axis=0, tiled=True)  17.9 us
    all_to_all x1, waiting for transfers between devices, send_back(): lax.all_to_all(results, 'ep', split_axis=0, concat_axis=0, tiled=True)  13.7 us
    all_gather x1, blocking collectives, shards(): lax.all_gather(routed.astype(jnp.bfloat16), 'ep', axis=0, tiled=True)  12.5 us
    dot_general x1, matrix products, run_experts(): jnp.einsum('scd,df->scf', arrived, gate_up, preferred_element_type=jnp.fl...  6.73 us
    ppermute x1, waiting for transfers between devices, from_behind(): lax.ppermute(shard, axis, [(i, (i + by) % devices) for i in range(devices)])  5.43 us
    dot_general x1, matrix products, run_experts(): jnp.einsum('scf,fd->scd', active, down_matrix, preferred_element_type=jnp...  5.3 us
    all_to_all x1, starting transfers between devices, send_back(): lax.all_to_all(results, 'ep', split_axis=0, concat_axis=0, tiled=True)  4.19 us
  transfers between devices with their start and end apart: 2, of which 2 were waited for; matrix products, arithmetic and copies ran while one was open for 1% of the time, Pallas kernels for 0%

commit v1 on v0

v1 whole, which is shorter than its diff:
```python
import functools

import jax
import jax.numpy as jnp
from jax import lax
from jax.experimental import pallas as pl
from jax.experimental.pallas import tpu as pltpu
from jax.sharding import PartitionSpec as P

EXPERTS = 4
TOP = 2
CAP = 24

guidance_scale = 2.5
epsilon = 1e-06
F32 = jnp.float32
BF16 = jnp.bfloat16
VMEM = pl.BlockSpec(memory_space=pltpu.VMEM)
SMEM = pl.BlockSpec(memory_space=pltpu.SMEM)


def chunk_of(extent, largest):
    size = largest
    while extent % size:
        size //= 2
    return size


def offset_target(me, offset, devices):
    if devices & (devices - 1) == 0:
        return me ^ offset
    return (me + offset) % devices


def route_kernel(devices, place, hidden, gain, ids, gates, partner, *outs):
    picked, mix = outs[:-1], outs[-1]
    rows, width = hidden.shape
    middle = rows // 2
    widened = hidden[...].astype(F32)
    factor = lax.rsqrt(jnp.mean(widened * widened, axis=-1, keepdims=True) + epsilon)
    normed = (widened * factor * gain[...].astype(F32)).astype(BF16)

    shards_each = devices // EXPERTS
    me, is_last = place[0], place[1]
    line = lax.broadcasted_iota(jnp.int32, (rows, rows), 0)
    lane = lax.broadcasted_iota(jnp.int32, (rows, rows), 1)
    before = (line < lane).astype(F32)
    expert = lax.broadcasted_iota(jnp.int32, (EXPERTS, rows), 0)
    named = jnp.zeros((EXPERTS, rows), F32)
    weight = jnp.zeros((EXPERTS, rows), F32)
    for k in range(TOP):
        same = ids[k : k + 1, :] == expert
        named = named + same.astype(F32)
        weight = weight + jnp.where(same, gates[k : k + 1, :], 0.0)
    position = jnp.dot(named, before, preferred_element_type=F32)
    position = jnp.where(named > 0.0, position, -1.0)

    slot = lax.broadcasted_iota(jnp.int32, (CAP, rows), 0).astype(F32)
    choices, weighted = [], [(line == lane).astype(F32)]
    for offset in range(devices):
        own = offset_target(me, offset, devices) // shards_each
        mine = expert == own
        where_to = jnp.sum(jnp.where(mine, position, 0.0), axis=0, keepdims=True)
        share = jnp.sum(jnp.where(mine, weight, 0.0), axis=0, keepdims=True)
        choice = (where_to == slot).astype(F32)
        choices.append(choice)
        weighted.append(choice * share)
    for offset in range(devices):
        picked[offset][...] = jnp.dot(
            choices[offset].astype(BF16), normed, preferred_element_type=F32
        ).astype(BF16)

    pair_line = lax.broadcasted_iota(jnp.int32, (rows, middle), 0)
    pair_lane = lax.broadcasted_iota(jnp.int32, (rows, middle), 1)
    pair = jnp.sum(
        jnp.where(pair_line == pair_lane, partner[...].astype(F32), 0.0), axis=1, keepdims=True
    )
    same_row = (line == lane).astype(F32)
    weak_row = (lane.astype(F32) == pair + float(middle)).astype(F32)
    guided = guidance_scale * same_row + (1.0 - guidance_scale) * weak_row
    guide = jnp.where(jnp.logical_and(line < middle, is_last > 0), guided, same_row)
    mix[...] = lax.dot_general(
        guide,
        jnp.concatenate(weighted, axis=0),
        (((1,), (1,)), ((), ())),
        precision=lax.Precision.HIGHEST,
        preferred_element_type=F32,
    )


def route(place, hidden, gain, ids, gates, partner, devices):
    rows, width = hidden.shape
    return pl.pallas_call(
        functools.partial(route_kernel, devices),
        out_shape=[jax.ShapeDtypeStruct((CAP, width), BF16)] * devices
        + [jax.ShapeDtypeStruct((rows, rows + devices * CAP), F32)],
        in_specs=[SMEM] + [VMEM] * 5,
        out_specs=[VMEM] * (devices + 1),
        compiler_params=pltpu.CompilerParams(vmem_limit_bytes=16 << 20),
    )(place, hidden, gain, ids, gates, partner)


def expert_kernel(count, step, *refs):
    rows = refs[:count]
    gate_up, down = refs[count : count + 2]
    outs = refs[count + 2 :]
    half = down.shape[0]
    stacked = jnp.concatenate([r[...].astype(F32) for r in rows], axis=0).astype(BF16)
    projected = jnp.dot(stacked, gate_up[...], preferred_element_type=F32)
    gate, up = projected[:, :half], projected[:, half:]
    active = (gate / (1.0 + jnp.exp(-gate)) * up).astype(BF16)

    def columns(i, carry):
        at = pl.ds(pl.multiple_of(i * step, step), step)
        part = jnp.dot(active, down[:, at], preferred_element_type=F32)
        for k in range(count):
            outs[k][:, at] = part[k * CAP : (k + 1) * CAP].astype(BF16)
        return carry

    lax.fori_loop(0, down.shape[1] // step, columns, 0)


def experts(rows, gate_up, down):
    count = len(rows)
    width = down.shape[1]
    total = count * CAP
    return pl.pallas_call(
        functools.partial(expert_kernel, count, chunk_of(width, 512)),
        out_shape=[jax.ShapeDtypeStruct((CAP, width), BF16)] * count,
        in_specs=[VMEM] * (count + 2),
        out_specs=[VMEM] * count,
        compiler_params=pltpu.CompilerParams(vmem_limit_bytes=(8 << 20) + total * width * 8),
        cost_estimate=pl.CostEstimate(
            flops=2 * total * (gate_up.size + down.size),
            bytes_accessed=2 * (gate_up.size + down.size),
            transcendentals=total * down.shape[0],
        ),
    )(*rows, gate_up, down)


def combine_kernel(count, step, mix, hidden, *refs):
    slots, out = refs[:count], refs[count]
    high = mix[...].astype(BF16)
    low = (mix[...] - high.astype(F32)).astype(BF16)

    def columns(i, carry):
        at = pl.ds(pl.multiple_of(i * step, step), step)
        stacked = jnp.concatenate(
            [hidden[:, at].astype(F32)] + [s[:, at].astype(F32) for s in slots], axis=0
        ).astype(BF16)
        out[:, at] = (
            jnp.dot(high, stacked, preferred_element_type=F32)
            + jnp.dot(low, stacked, preferred_element_type=F32)
        ).astype(BF16)
        return carry

    lax.fori_loop(0, out.shape[1] // step, columns, 0)


def combine(mix, hidden, slots):
    count = len(slots)
    rows, width = hidden.shape
    return pl.pallas_call(
        functools.partial(combine_kernel, count, chunk_of(width, 512)),
        out_shape=jax.ShapeDtypeStruct((rows, width), BF16),
        in_specs=[VMEM] * (count + 2),
        out_specs=VMEM,
        compiler_params=pltpu.CompilerParams(vmem_limit_bytes=16 << 20),
    )(mix, hidden, *slots)


def shards(hidden, norm_gain, expert_ids, gate_weights, expert_gate_up, expert_down, partner):
    devices = lax.axis_size("ep")
    sections = lax.axis_size("pp")
    place = jnp.stack(
        [lax.axis_index("ep"), (lax.axis_index("pp") == sections - 1).astype(jnp.int32)]
    )
    section_rows = hidden[0]
    gate_up = expert_gate_up[0, 0]
    down = expert_down[0, 0]

    *picked, mix = route(
        place, section_rows, norm_gain, expert_ids[0].T, gate_weights[0].T, partner, devices
    )

    def onward(value):
        return lax.ppermute(value, "pp", [(i, (i + 1) % sections) for i in range(sections)])

    def dispatch(value, offset):
        if offset == 0:
            return value
        return lax.ppermute(
            value, "ep", [(i, offset_target(i, offset, devices)) for i in range(devices)]
        )

    def send_back(value, offset):
        return lax.ppermute(
            value,
            ("ep", "pp"),
            [
                (offset_target(i, offset, devices) * sections + p, i * sections + (p + 1) % sections)
                for i in range(devices)
                for p in range(sections)
            ],
        )

    split = max(1, devices * 3 // 4)
    order = [devices // 2] + [k for k in range(split, devices)]
    order += [k for k in range(devices) if k not in order]
    arrived = {}
    for k in order:
        arrived[k] = dispatch(picked[k], k)
    hidden_before = onward(section_rows)
    mix_before = onward(mix)

    returned = {}
    for group in (range(0, split), range(split, devices)):
        if len(group):
            results = experts([arrived[k] for k in group], gate_up, down)
            for k in sorted(group, key=lambda j: order.index(j)):
                returned[k] = send_back(results[k - group[0]], k)
    out = combine(mix_before, hidden_before, [returned[k] for k in range(devices)])
    return out[None]


def solution(mesh):
    return jax.shard_map(
        shards,
        mesh=mesh,
        in_specs=(
            P("pp", ("grp", "ep"), None),
            P("pp", None),
            P("pp", ("grp", "ep"), None),
            P("pp", ("grp", "ep"), None),
            P("pp", "ep", None, None),
            P("pp", "ep", None, None),
            P(("grp", "ep"), None),
        ),
        out_specs=P("pp", ("grp", "ep"), None),
        check_vma=False,
    )
```

time: 76.2 us -> 56.1 us (0.74)
  the two profiles are of different devices: /device:TPU:0 before, /device:TPU:9 now
where the time goes in v1:
time: 56.1 us; the launch traced here: 55.5 us
  starting transfers between devices  16 us (29%)
  waiting for transfers between devices  15.6 us (28%)
  Pallas kernels  12.9 us (23%)
  local copies, waits for them, and re-layouts  11 us (20%)
    unnamed x16, local copies, waits for them, and re-layouts  11 us
    ppermute x4, waiting for transfers between devices, send_back(): lax.ppermute(value, ('ep', 'pp'), [(offset_target(i, offset, devices) * s...  10.9 us
    ppermute x4, starting transfers between devices, send_back(): lax.ppermute(value, ('ep', 'pp'), [(offset_target(i, offset, devices) * s...  10.7 us
    pallas_call x2, Pallas kernels, experts(): pl.pallas_call(functools.partial(expert_kernel, count, chunk_of(width, 51...  9.43 us
    ppermute x3, waiting for transfers between devices, dispatch(): lax.ppermute(value, 'ep', [(i, offset_target(i, offset, devices)) for i i...  4.69 us
    ppermute x3, starting transfers between devices, dispatch(): lax.ppermute(value, 'ep', [(i, offset_target(i, offset, devices)) for i i...  2.65 us
    ppermute x2, starting transfers between devices, onward(): lax.ppermute(value, 'pp', [(i, (i + 1) % sections) for i in range(section...  2.64 us
    pallas_call x1, Pallas kernels, combine(): pl.pallas_call(functools.partial(combine_kernel, count, chunk_of(width, 5...  1.86 us
  transfers between devices with their start and end apart: 9, of which 4 were waited for; matrix products, arithmetic and copies ran while one was open for 0% of the time, Pallas kernels for 17%

profile of v1, /device:TPU:9, one launch (start us, length us, event | category | flops | bytes accessed | tf_op | source)
XLA Modules:
  0.0 55.5 jit_solution(7021541792912342672)
XLA Ops:
  0.0 0.1 pad_add_fusion.place
  0.1 0.0 copy-start.4
  0.1 0.7 %copy-done.4 = bf16[1,3584]{1,0:T(2,128)(2,1)S(1)} copy-done((bf16[1,3584]{1,0:T(2,128)(2,1)S(1)}, bf16[1,3584]{1,0:T(2,128)(2,1)}, u32[]{:S(2)}) %copy-start.4) | copy-done | bytes 7192
  0.8 0.7 %copy-done.5 = s32[1,32,2]{1,2,0:T(2,128)S(1)} copy-done((s32[1,32,2]{1,2,0:T(2,128)S(1)}, s32[1,32,2]{1,2,0:T(2,128)}, u32[]{:S(2)}) %copy-start.5) | copy-done | bytes 280
  1.5 0.7 %copy-done.6 = f32[1,32,2]{1,2,0:T(2,128)S(1)} copy-done((f32[1,32,2]{1,2,0:T(2,128)S(1)}, f32[1,32,2]{1,2,0:T(2,128)}, u32[]{:S(2)}) %copy-start.6) | copy-done | bytes 280
  2.1 0.7 %copy-done.7 = s32[1,16]{1,0:T(1,128)S(1)} copy-done((s32[1,16]{1,0:T(1,128)S(1)}, s32[1,16]{1,0:T(1,128)}, u32[]{:S(2)}) %copy-start.7) | copy-done | bytes 88
  2.8 1.6 %shard_map.73 = (bf16[24,3584]{1,0:T(8,128)(2,1)S(1)}, bf16[24,3584]{1,0:T(8,128)(2,1)S(1)}, bf16[24,3584]{1,0:T(8,128)(2,1)S(1)}, bf16[24,3584]{1,0:T(8,128)(2,1)S(1)}, f32[32,128]{1,0:T(8,128)S(1)}) custom-call(s32[2]{0:T(128)S(1)} %pad_add_fusion.place, bf16[32,3584]{1,0:T(8,128)(2,1)} %bitcast.2.hidden, bf16[1,3584]{1,0:T(2,128)(2,1)S(1)} %copy-done.4, ...), custom_call_target="tpu_custom_call" | custom-call | tf_op jit(solution)/shard_map/pallas_call | solution.py:93
  4.4 0.0 collective-permute-start.2
  4.4 2.5 %collective-permute-start.3 = (bf16[24,3584]{1,0:T(8,128)(2,1)S(1)}, bf16[24,3584]{1,0:T(8,128)(2,1)S(1)}, u32[]{:S(2)}, u32[]{:S(2)}) collective-permute-start(bf16[24,3584]{1,0:T(8,128)(2,1)S(1)} %get-tuple-element.16), channel_id=1, source_target_pairs={{0,8},{4,12},{8,0},{12,4},{1,9},{5,13},{9,1},{13,5},{2,10},{6,14},... | collective-permute-start | bytes 516104 | tf_op jit(solution)/shard_map/ppermute | solution.py:192
  6.9 0.2 collective-permute-start.7
  7.0 2.6 %collective-permute-start.1 = (bf16[32,3584]{1,0:T(8,128)(2,1)}, bf16[32,3584]{1,0:T(8,128)(2,1)S(1)}, u32[]{:S(2)}, u32[]{:S(2)}) collective-permute-start(bf16[32,3584]{1,0:T(8,128)(2,1)} %bitcast.2.hidden), channel_id=1, source_target_pairs={{0,1},{1,2},{2,3},{3,0},{4,5},{5,6},{6,7},{7,4},{8,9},{9,10},{10,1... | collective-permute-start | bytes 688136 | tf_op jit(solution)/shard_map/ppermute | solution.py:187
  9.6 0.0 collective-permute-start
  9.7 0.2 collective-permute-done.2.refs_1_
  9.9 4.5 %collective-permute-done.3.refs_2_ = bf16[24,3584]{1,0:T(8,128)(2,1)S(1)} collective-permute-done((bf16[24,3584]{1,0:T(8,128)(2,1)S(1)}, bf16[24,3584]{1,0:T(8,128)(2,1)S(1)}, u32[]{:S(2)}, u32[]{:S(2)}) %collective-permute-start.3) | collective-permute-done | bytes 172064 | tf_op jit(solution)/shard_map/ppermute | solution.py:192
  14.4 5.2 %copy-done = bf16[1,1,3584,2048]{3,2,1,0:T(8,128)(2,1)S(1)} copy-done((bf16[1,1,3584,2048]{3,2,1,0:T(8,128)(2,1)S(1)}, bf16[1,1,3584,2048]{3,2,1,0:T(8,128)(2,1)}, u32[]{:S(2)}) %copy-start) | copy-done | bytes 14680088
  19.5 3.1 %copy-done.2 = bf16[1,1,1024,3584]{3,2,1,0:T(8,128)(2,1)S(1)} copy-done((bf16[1,1,1024,3584]{3,2,1,0:T(8,128)(2,1)S(1)}, bf16[1,1,1024,3584]{3,2,1,0:T(8,128)(2,1)}, u32[]{:S(2)}) %copy-start.2) | copy-done | bytes 7340056
  22.6 4.8 %shard_map.74 = (bf16[24,3584]{1,0:T(8,128)(2,1)S(1)}, bf16[24,3584]{1,0:T(8,128)(2,1)S(1)}, bf16[24,3584]{1,0:T(8,128)(2,1)S(1)}) custom-call(bf16[24,3584]{1,0:T(8,128)(2,1)S(1)} %get-tuple-element.14.refs_0_, bf16[24,3584]{1,0:T(8,128)(2,1)S(1)} %collective-permute-done.2.refs_1_, bf16[24,3584]{1,0:T(8,128)(2,1)S(1)} %collective-permute-done.3.refs_2_, ...), custom_call_target="tpu_custom_call" | custom-call | flops 1585446912 | bytes 22020096 | tf_op jit(solution)/shard_map/pallas_call | solution.py:127
  27.4 7.0 %collective-permute-start.4 = (bf16[24,3584]{1,0:T(8,128)(2,1)S(1)}, bf16[24,3584]{1,0:T(8,128)(2,1)S(1)}, u32[]{:S(2)}, u32[]{:S(2)}) collective-permute-start(bf16[24,3584]{1,0:T(8,128)(2,1)S(1)} %get-tuple-element.17), channel_id=1, source_target_pairs={{0,1},{1,2},{2,3},{3,0},{4,5},{5,6},{6,7},{7,4},{8,9},{9,10},{10,1... | collective-permute-start | bytes 516104 | tf_op jit(solution)/shard_map/ppermute | solution.py:197
  34.4 2.0 %collective-permute-start.5 = (bf16[24,3584]{1,0:T(8,128)(2,1)S(1)}, bf16[24,3584]{1,0:T(8,128)(2,1)S(1)}, u32[]{:S(2)}, u32[]{:S(2)}) collective-permute-start(bf16[24,3584]{1,0:T(8,128)(2,1)S(1)} %get-tuple-element.18), channel_id=1, source_target_pairs={{4,1},{5,2},{6,3},{7,0},{0,5},{1,6},{2,7},{3,4},{12,9},{13,10},{14... | collective-permute-start | bytes 516104 | tf_op jit(solution)/shard_map/ppermute | solution.py:197
  36.4 0.0 collective-permute-done.7.refs_0_
  36.4 1.0 %collective-permute-start.6 = (bf16[24,3584]{1,0:T(8,128)(2,1)S(1)}, bf16[24,3584]{1,0:T(8,128)(2,1)S(1)}, u32[]{:S(2)}, u32[]{:S(2)}) collective-permute-start(bf16[24,3584]{1,0:T(8,128)(2,1)S(1)} %get-tuple-element.19), channel_id=1, source_target_pairs={{8,1},{9,2},{10,3},{11,0},{12,5},{13,6},{14,7},{15,4},{0,9},{1,10}... | collective-permute-start | bytes 516104 | tf_op jit(solution)/shard_map/ppermute | solution.py:197
  37.4 0.0 copy-done.1
  37.4 0.0 copy-done.3
  37.4 4.6 %shard_map.75 = bf16[24,3584]{1,0:T(8,128)(2,1)S(1)} custom-call(bf16[24,3584]{1,0:T(8,128)(2,1)S(1)} %collective-permute-done.7.refs_0_, bf16[3584,2048]{1,0:T(8,128)(2,1)S(1)} %bitcast.13, bf16[1024,3584]{1,0:T(8,128)(2,1)S(1)} %bitcast.15), custom_call_target="tpu_custom_call" | custom-call | flops 528482304 | bytes 22020096 | tf_op jit(solution)/shard_map/pallas_call | solution.py:127
  42.0 0.0 collective-permute-done.mix
  42.0 0.7 %collective-permute-start.8 = (bf16[24,3584]{1,0:T(8,128)(2,1)S(1)}, bf16[24,3584]{1,0:T(8,128)(2,1)S(1)}, u32[]{:S(2)}, u32[]{:S(2)}) collective-permute-start(bf16[24,3584]{1,0:T(8,128)(2,1)S(1)} %shard_map.75), channel_id=1, source_target_pairs={{12,1},{13,2},{14,3},{15,0},{8,5},{9,6},{10,7},{11,4},{4,9},{5,10}... | collective-permute-start | bytes 516104 | tf_op jit(solution)/shard_map/ppermute | solution.py:197
  42.8 0.0 collective-permute-done.1.hidden
  42.8 0.0 collective-permute-done.4.refs_0_
  42.8 0.0 collective-permute-done.5.refs_1_
  42.8 1.8 %collective-permute-done.6.refs_2_ = bf16[24,3584]{1,0:T(8,128)(2,1)S(1)} collective-permute-done((bf16[24,3584]{1,0:T(8,128)(2,1)S(1)}, bf16[24,3584]{1,0:T(8,128)(2,1)S(1)}, u32[]{:S(2)}, u32[]{:S(2)}) %collective-permute-start.6) | collective-permute-done | bytes 172064 | tf_op jit(solution)/shard_map/ppermute | solution.py:197
  44.5 9.1 %collective-permute-done.8.refs_3_ = bf16[24,3584]{1,0:T(8,128)(2,1)S(1)} collective-permute-done((bf16[24,3584]{1,0:T(8,128)(2,1)S(1)}, bf16[24,3584]{1,0:T(8,128)(2,1)S(1)}, u32[]{:S(2)}, u32[]{:S(2)}) %collective-permute-start.8) | collective-permute-done | bytes 172064 | tf_op jit(solution)/shard_map/ppermute | solution.py:197
  53.7 1.9 %shard_map.76 = bf16[32,3584]{1,0:T(8,128)(2,1)} custom-call(f32[32,128]{1,0:T(8,128)S(1)} %collective-permute-done.mix, bf16[32,3584]{1,0:T(8,128)(2,1)S(1)} %collective-permute-done.1.hidden, bf16[24,3584]{1,0:T(8,128)(2,1)S(1)} %collective-permute-done.4.refs_0_, bf16[24,3584]{1,0:T(8,128)(2,1)S(1)} %collective-permute-done.5.refs_1_, ...), custom_call_target="tpu_custom_call" | custom-call | tf_op jit(solution)/shard_map/pallas_call | solution.py:163
  (7 shorter events, 0.0 us)
Async XLA Ops:
  0.1 0.7 %copy-start.4 = (bf16[1,3584]{1,0:T(2,128)(2,1)S(1)}, bf16[1,3584]{1,0:T(2,128)(2,1)}, u32[]{:S(2)}) copy-start(bf16[1,3584]{1,0:T(2,128)(2,1)} %gain.1) | copy-start | bytes 21508
  0.8 0.7 %copy-start.5 = (s32[1,32,2]{1,2,0:T(2,128)S(1)}, s32[1,32,2]{1,2,0:T(2,128)}, u32[]{:S(2)}) copy-start(s32[1,32,2]{1,2,0:T(2,128)} %param.9) | copy-start | bytes 772
  1.5 0.7 %copy-start.6 = (f32[1,32,2]{1,2,0:T(2,128)S(1)}, f32[1,32,2]{1,2,0:T(2,128)}, u32[]{:S(2)}) copy-start(f32[1,32,2]{1,2,0:T(2,128)} %param.10) | copy-start | bytes 772
  2.1 0.7 %copy-start.7 = (s32[1,16]{1,0:T(1,128)S(1)}, s32[1,16]{1,0:T(1,128)}, u32[]{:S(2)}) copy-start(s32[1,16]{1,0:T(1,128)} %partner.1) | copy-start | bytes 196
  4.4 5.5 %collective-permute-start.2 = (bf16[24,3584]{1,0:T(8,128)(2,1)S(1)}, bf16[24,3584]{1,0:T(8,128)(2,1)S(1)}, u32[]{:S(2)}, u32[]{:S(2)}) collective-permute-start(bf16[24,3584]{1,0:T(8,128)(2,1)S(1)} %get-tuple-element.15), channel_id=1, source_target_pairs={{0,4},{4,0},{8,12},{12,8},{1,5},{5,1},{9,13},{13,9},{2,6},{6,2},{1... | collective-permute-start | bytes 516104 | tf_op jit(solution)/shard_map/ppermute | solution.py:192
  4.4 10.0 %collective-permute-start.3 = (bf16[24,3584]{1,0:T(8,128)(2,1)S(1)}, bf16[24,3584]{1,0:T(8,128)(2,1)S(1)}, u32[]{:S(2)}, u32[]{:S(2)}) collective-permute-start(bf16[24,3584]{1,0:T(8,128)(2,1)S(1)} %get-tuple-element.16), channel_id=1, source_target_pairs={{0,8},{4,12},{8,0},{12,4},{1,9},{5,13},{9,1},{13,5},{2,10},{6,14},... | collective-permute-start | bytes 516104 | tf_op jit(solution)/shard_map/ppermute | solution.py:192
  6.9 29.5 %collective-permute-start.7 = (bf16[24,3584]{1,0:T(8,128)(2,1)S(1)}, bf16[24,3584]{1,0:T(8,128)(2,1)S(1)}, u32[]{:S(2)}, u32[]{:S(2)}) collective-permute-start(bf16[24,3584]{1,0:T(8,128)(2,1)S(1)} %get-tuple-element.20), channel_id=1, source_target_pairs={{0,12},{4,8},{8,4},{12,0},{1,13},{5,9},{9,5},{13,1},{2,14},{6,10},... | collective-permute-start | bytes 516104 | tf_op jit(solution)/shard_map/ppermute | solution.py:192
  7.0 35.7 %collective-permute-start.1 = (bf16[32,3584]{1,0:T(8,128)(2,1)}, bf16[32,3584]{1,0:T(8,128)(2,1)S(1)}, u32[]{:S(2)}, u32[]{:S(2)}) collective-permute-start(bf16[32,3584]{1,0:T(8,128)(2,1)} %bitcast.2.hidden), channel_id=1, source_target_pairs={{0,1},{1,2},{2,3},{3,0},{4,5},{5,6},{6,7},{7,4},{8,9},{9,10},{10,1... | collective-permute-start | bytes 688136 | tf_op jit(solution)/shard_map/ppermute | solution.py:187
  9.6 32.4 %collective-permute-start = (f32[32,128]{1,0:T(8,128)S(1)}, f32[32,128]{1,0:T(8,128)S(1)}, u32[]{:S(2)}, u32[]{:S(2)}) collective-permute-start(f32[32,128]{1,0:T(8,128)S(1)} %get-tuple-element.13), channel_id=1, source_target_pairs={{0,1},{1,2},{2,3},{3,0},{4,5},{5,6},{6,7},{7,4},{8,9},{9,10},{10,1... | collective-permute-start | bytes 49160 | tf_op jit(solution)/shard_map/ppermute | solution.py:187
  14.4 5.2 %copy-start = (bf16[1,1,3584,2048]{3,2,1,0:T(8,128)(2,1)S(1)}, bf16[1,1,3584,2048]{3,2,1,0:T(8,128)(2,1)}, u32[]{:S(2)}) copy-start(bf16[1,1,3584,2048]{3,2,1,0:T(8,128)(2,1)} %param.11) | copy-start | bytes 44040196
  19.5 3.1 %copy-start.2 = (bf16[1,1,1024,3584]{3,2,1,0:T(8,128)(2,1)S(1)}, bf16[1,1,1024,3584]{3,2,1,0:T(8,128)(2,1)}, u32[]{:S(2)}) copy-start(bf16[1,1,1024,3584]{3,2,1,0:T(8,128)(2,1)} %param.12) | copy-start | bytes 22020100
  22.6 14.8 %copy-start.1 = (bf16[1,1,3584,2048]{3,2,1,0:T(8,128)(2,1)S(1)}, bf16[1,1,3584,2048]{3,2,1,0:T(8,128)(2,1)}, u32[]{:S(2)}) copy-start(bf16[1,1,3584,2048]{3,2,1,0:T(8,128)(2,1)} %param.11) | copy-start | bytes 44040196
  22.6 14.8 %copy-start.3 = (bf16[1,1,1024,3584]{3,2,1,0:T(8,128)(2,1)S(1)}, bf16[1,1,1024,3584]{3,2,1,0:T(8,128)(2,1)}, u32[]{:S(2)}) copy-start(bf16[1,1,1024,3584]{3,2,1,0:T(8,128)(2,1)} %param.12) | copy-start | bytes 22020100
  27.4 15.3 %collective-permute-start.4 = (bf16[24,3584]{1,0:T(8,128)(2,1)S(1)}, bf16[24,3584]{1,0:T(8,128)(2,1)S(1)}, u32[]{:S(2)}, u32[]{:S(2)}) collective-permute-start(bf16[24,3584]{1,0:T(8,128)(2,1)S(1)} %get-tuple-element.17), channel_id=1, source_target_pairs={{0,1},{1,2},{2,3},{3,0},{4,5},{5,6},{6,7},{7,4},{8,9},{9,10},{10,1... | collective-permute-start | bytes 516104 | tf_op jit(solution)/shard_map/ppermute | solution.py:197
  34.4 8.3 %collective-permute-start.5 = (bf16[24,3584]{1,0:T(8,128)(2,1)S(1)}, bf16[24,3584]{1,0:T(8,128)(2,1)S(1)}, u32[]{:S(2)}, u32[]{:S(2)}) collective-permute-start(bf16[24,3584]{1,0:T(8,128)(2,1)S(1)} %get-tuple-element.18), channel_id=1, source_target_pairs={{4,1},{5,2},{6,3},{7,0},{0,5},{1,6},{2,7},{3,4},{12,9},{13,10},{14... | collective-permute-start | bytes 516104 | tf_op jit(solution)/shard_map/ppermute | solution.py:197
  36.4 8.2 %collective-permute-start.6 = (bf16[24,3584]{1,0:T(8,128)(2,1)S(1)}, bf16[24,3584]{1,0:T(8,128)(2,1)S(1)}, u32[]{:S(2)}, u32[]{:S(2)}) collective-permute-start(bf16[24,3584]{1,0:T(8,128)(2,1)S(1)} %get-tuple-element.19), channel_id=1, source_target_pairs={{8,1},{9,2},{10,3},{11,0},{12,5},{13,6},{14,7},{15,4},{0,9},{1,10}... | collective-permute-start | bytes 516104 | tf_op jit(solution)/shard_map/ppermute | solution.py:197
  42.0 11.7 %collective-permute-start.8 = (bf16[24,3584]{1,0:T(8,128)(2,1)S(1)}, bf16[24,3584]{1,0:T(8,128)(2,1)S(1)}, u32[]{:S(2)}, u32[]{:S(2)}) collective-permute-start(bf16[24,3584]{1,0:T(8,128)(2,1)S(1)} %shard_map.75), channel_id=1, source_target_pairs={{12,1},{13,2},{14,3},{15,0},{8,5},{9,6},{10,7},{11,4},{4,9},{5,10}... | collective-permute-start | bytes 516104 | tf_op jit(solution)/shard_map/ppermute | solution.py:197

commit v2 on v1

v2 whole, which is shorter than its diff:
```python
import functools

import jax
import jax.numpy as jnp
from jax import lax
from jax.experimental import pallas as pl
from jax.experimental.pallas import tpu as pltpu
from jax.sharding import PartitionSpec as P

EXPERTS = 4
TOP = 2
CAP = 24

guidance_scale = 2.5
epsilon = 1e-06
F32 = jnp.float32
BF16 = jnp.bfloat16
VMEM = pl.BlockSpec(memory_space=pltpu.VMEM)
SMEM = pl.BlockSpec(memory_space=pltpu.SMEM)
HBM = pl.BlockSpec(memory_space=pltpu.HBM)


def chunk_of(extent, largest):
    size = largest
    while extent % size:
        size //= 2
    return size


def in_hbm(*arrays):
    return [pltpu.with_memory_space_constraint(a, pltpu.HBM) for a in arrays]


def lanes_for(extent):
    return -(-extent // 128) * 128


def offset_target(me, offset, devices):
    if devices & (devices - 1) == 0:
        return me ^ offset
    return (me + offset) % devices


def fetch(pairs, sems):
    copies = [pltpu.make_async_copy(s, d, sems.at[i]) for i, (s, d) in enumerate(pairs)]
    for copy in copies:
        copy.start()
    for copy in copies:
        copy.wait()


def slot_positions(ids, rows):
    line = lax.broadcasted_iota(jnp.int32, (rows, rows), 0)
    lane = lax.broadcasted_iota(jnp.int32, (rows, rows), 1)
    expert = lax.broadcasted_iota(jnp.int32, (EXPERTS, rows), 0)
    named = jnp.zeros((EXPERTS, rows), F32)
    for k in range(TOP):
        named = named + (ids[k : k + 1, :] == expert).astype(F32)
    position = jnp.dot(named, (line < lane).astype(F32), preferred_element_type=F32)
    return jnp.where(named > 0.0, position, -1.0)


def of_expert(table, own):
    expert = lax.broadcasted_iota(jnp.int32, table.shape, 0)
    return jnp.sum(jnp.where(expert == own, table, 0.0), axis=0, keepdims=True)


def choice_of(position, own, rows):
    slot = lax.broadcasted_iota(jnp.int32, (CAP, rows), 0).astype(F32)
    return (of_expert(position, own) == slot).astype(F32)


def pick(choice, normed):
    return jnp.dot(choice.astype(BF16), normed, preferred_element_type=F32).astype(BF16)


def first_kernel(devices, offset, place, hidden_at, gain_at, ids_at, picked, normed, hidden, gain, ids, sems):
    fetch([(ids_at, ids), (gain_at, gain), (hidden_at, hidden)], sems)
    rows, _ = hidden.shape
    own = offset_target(place[0], offset, devices) // (devices // EXPERTS)
    choice = choice_of(slot_positions(ids, rows), own, rows)
    widened = hidden[...].astype(F32)
    factor = lax.rsqrt(jnp.mean(widened * widened, axis=-1, keepdims=True) + epsilon)
    normed[...] = (widened * factor * gain[...].astype(F32)).astype(BF16)
    picked[...] = pick(choice, normed[...])


def route_first(place, hidden, gain, ids, devices, offset):
    rows, width = hidden.shape
    return pl.pallas_call(
        functools.partial(first_kernel, devices, offset),
        out_shape=[
            jax.ShapeDtypeStruct((CAP, width), BF16),
            jax.ShapeDtypeStruct((rows, width), BF16),
        ],
        in_specs=[SMEM] + [HBM] * 3,
        out_specs=[VMEM] * 2,
        scratch_shapes=[
            pltpu.VMEM(hidden.shape, BF16),
            pltpu.VMEM(gain.shape, BF16),
            pltpu.VMEM(ids.shape, jnp.int32),
            pltpu.SemaphoreType.DMA((3,)),
        ],
        compiler_params=pltpu.CompilerParams(vmem_limit_bytes=8 << 20),
    )(place, *in_hbm(hidden, gain, ids))


def rest_kernel(devices, offsets, place, normed, hidden_at, ids_at, gates_at, partner_at, *refs):
    picked, packed = refs[: len(offsets)], refs[len(offsets)]
    ids, gates, partner, sems = refs[len(offsets) + 1 :]
    rows, width = normed.shape
    fetch(
        [
            (ids_at, ids),
            (gates_at, gates),
            (partner_at, partner),
            (hidden_at, packed.at[:, pl.ds(0, width)]),
        ],
        sems,
    )
    middle = rows // 2
    me, is_last = place[0], place[1]
    position = slot_positions(ids, rows)
    expert = lax.broadcasted_iota(jnp.int32, (EXPERTS, rows), 0)
    weight = jnp.zeros((EXPERTS, rows), F32)
    for k in range(TOP):
        weight = weight + jnp.where(ids[k : k + 1, :] == expert, gates[k : k + 1, :], 0.0)

    line = lax.broadcasted_iota(jnp.int32, (rows, rows), 0)
    lane = lax.broadcasted_iota(jnp.int32, (rows, rows), 1)
    same_row = (line == lane).astype(F32)
    weighted = [same_row]
    for offset in range(devices):
        own = offset_target(me, offset, devices) // (devices // EXPERTS)
        choice = choice_of(position, own, rows)
        weighted.append(choice * of_expert(weight, own))
        if offset in offsets:
            picked[offsets.index(offset)][...] = pick(choice, normed[...])

    pair_line = lax.broadcasted_iota(jnp.int32, (rows, middle), 0)
    pair_lane = lax.broadcasted_iota(jnp.int32, (rows, middle), 1)
    pair = jnp.sum(
        jnp.where(pair_line == pair_lane, partner[...].astype(F32), 0.0), axis=1, keepdims=True
    )
    weak_row = (lane.astype(F32) == pair + float(middle)).astype(F32)
    guided = guidance_scale * same_row + (1.0 - guidance_scale) * weak_row
    guide = jnp.where(jnp.logical_and(line < middle, is_last > 0), guided, same_row)
    span = (packed.shape[1] - width) // 2
    if span > rows + devices * CAP:
        weighted.append(jnp.zeros((span - rows - devices * CAP, rows), F32))
    mix = lax.dot_general(
        guide,
        jnp.concatenate(weighted, axis=0),
        (((1,), (1,)), ((), ())),
        precision=lax.Precision.HIGHEST,
        preferred_element_type=F32,
    )
    high = mix.astype(BF16)
    packed[:, width : width + span] = high
    packed[:, width + span :] = (mix - high.astype(F32)).astype(BF16)


def route_rest(place, normed, hidden, ids, gates, partner, devices, offsets):
    rows, width = normed.shape
    span = lanes_for(rows + devices * CAP)
    return pl.pallas_call(
        functools.partial(rest_kernel, devices, offsets),
        out_shape=[jax.ShapeDtypeStruct((CAP, width), BF16)] * len(offsets)
        + [jax.ShapeDtypeStruct((rows, width + 2 * span), BF16)],
        in_specs=[SMEM, VMEM] + [HBM] * 4,
        out_specs=[VMEM] * (len(offsets) + 1),
        scratch_shapes=[
            pltpu.VMEM(ids.shape, jnp.int32),
            pltpu.VMEM(gates.shape, F32),
            pltpu.VMEM(partner.shape, jnp.int32),
            pltpu.SemaphoreType.DMA((4,)),
        ],
        compiler_params=pltpu.CompilerParams(vmem_limit_bytes=8 << 20),
    )(place, normed, *in_hbm(hidden, ids, gates, partner))


def load_kernel(parts, source, held, sems):
    size = source.shape[0] // parts
    fetch(
        [(source.at[pl.ds(i * size, size)], held.at[pl.ds(i * size, size)]) for i in range(parts)],
        sems,
    )


def load(matrix):
    parts = 7 if matrix.shape[0] % 112 == 0 else 1
    return pl.pallas_call(
        functools.partial(load_kernel, parts),
        out_shape=pltpu.VMEM(matrix.shape, matrix.dtype),
        in_specs=[HBM],
        out_specs=VMEM,
        scratch_shapes=[pltpu.SemaphoreType.DMA((parts,))],
        compiler_params=pltpu.CompilerParams(vmem_limit_bytes=1 << 20),
        cost_estimate=pl.CostEstimate(
            flops=0, bytes_accessed=2 * matrix.size, transcendentals=0
        ),
    )(*in_hbm(matrix))


def expert_kernel(count, step, loads, *refs):
    rows = refs[:count]
    gate_up, down = refs[count : count + 2]
    outs = refs[count + 2 : 2 * count + 2]
    if loads:
        held, sem = refs[2 * count + 2 :]
        copy = pltpu.make_async_copy(down, held, sem)
        copy.start()
    half = down.shape[0]
    stacked = jnp.concatenate([r[...].astype(F32) for r in rows], axis=0).astype(BF16)
    projected = jnp.dot(stacked, gate_up[...], preferred_element_type=F32)
    gate, up = projected[:, :half], projected[:, half:]
    active = (gate / (1.0 + jnp.exp(-gate)) * up).astype(BF16)
    if loads:
        copy.wait()
    else:
        held = down

    def columns(i, carry):
        at = pl.ds(pl.multiple_of(i * step, step), step)
        part = jnp.dot(active, held[:, at], preferred_element_type=F32)
        for k in range(count):
            outs[k][:, at] = part[k * CAP : (k + 1) * CAP].astype(BF16)
        return carry

    lax.fori_loop(0, down.shape[1] // step, columns, 0)


def experts(rows, gate_up, down, loads):
    count = len(rows)
    width = down.shape[1]
    total = count * CAP
    return pl.pallas_call(
        functools.partial(expert_kernel, count, chunk_of(width, 512), loads),
        out_shape=[jax.ShapeDtypeStruct((CAP, width), BF16)] * count
        + [pltpu.VMEM(down.shape, down.dtype)] * loads,
        in_specs=[VMEM] * (count + 1) + [HBM if loads else VMEM],
        out_specs=[VMEM] * (count + loads),
        scratch_shapes=[pltpu.SemaphoreType.DMA] * loads,
        compiler_params=pltpu.CompilerParams(vmem_limit_bytes=(6 << 20) + total * width * 8),
        cost_estimate=pl.CostEstimate(
            flops=2 * total * (gate_up.size + down.size),
            bytes_accessed=2 * (gate_up.size + down.size),
            transcendentals=total * down.shape[0],
        ),
    )(*rows, gate_up, *(in_hbm(down) if loads else [down]))


def combine_kernel(count, step, packed, *refs):
    slots, out = refs[:count], refs[count]
    rows, width = out.shape
    span = (packed.shape[1] - width) // 2
    used = rows + count * CAP
    high = packed[:, width : width + span][:, :used]
    low = packed[:, width + span :][:, :used]

    def columns(i, carry):
        at = pl.ds(pl.multiple_of(i * step, step), step)
        stacked = jnp.concatenate(
            [packed[:, at].astype(F32)] + [s[:, at].astype(F32) for s in slots], axis=0
        ).astype(BF16)
        out[:, at] = (
            jnp.dot(high, stacked, preferred_element_type=F32)
            + jnp.dot(low, stacked, preferred_element_type=F32)
        ).astype(BF16)
        return carry

    lax.fori_loop(0, width // step, columns, 0)


def combine(packed, slots):
    count = len(slots)
    rows, width = packed.shape[0], slots[0].shape[1]
    return pl.pallas_call(
        functools.partial(combine_kernel, count, chunk_of(width, 512)),
        out_shape=jax.ShapeDtypeStruct((rows, width), BF16),
        in_specs=[VMEM] * (count + 1),
        out_specs=VMEM,
        compiler_params=pltpu.CompilerParams(vmem_limit_bytes=8 << 20),
    )(packed, *slots)


def shards(hidden, norm_gain, expert_ids, gate_weights, expert_gate_up, expert_down, partner):
    devices = lax.axis_size("ep")
    sections = lax.axis_size("pp")
    place = jnp.stack(
        [lax.axis_index("ep"), (lax.axis_index("pp") == sections - 1).astype(jnp.int32)]
    )
    section_rows = hidden[0]
    gate_up = expert_gate_up[0, 0]
    down = expert_down[0, 0]

    far = devices // 2
    others = [k for k in range(devices - 1, -1, -1) if k != far]
    ids, gates = expert_ids[0].T, gate_weights[0].T
    picked = {}
    picked[far], normed = route_first(place, section_rows, norm_gain, ids, devices, far)
    *rest, packed = route_rest(
        place, normed, section_rows, ids, gates, partner, devices, others
    )
    picked.update(zip(others, rest))

    def onward(value):
        return lax.ppermute(value, "pp", [(i, (i + 1) % sections) for i in range(sections)])

    def dispatch(value, offset):
        if offset == 0:
            return value
        return lax.ppermute(
            value, "ep", [(i, offset_target(i, offset, devices)) for i in range(devices)]
        )

    def send_back(value, offset):
        return lax.ppermute(
            value,
            ("ep", "pp"),
            [
                (offset_target(i, offset, devices) * sections + p, i * sections + (p + 1) % sections)
                for i in range(devices)
                for p in range(sections)
            ],
        )

    arrived = {k: dispatch(picked[k], k) for k in [far] + others}
    gate_up = load(gate_up)
    packed, gate_up = lax.optimization_barrier((packed, gate_up))
    packed = onward(packed)

    split = max(1, devices * 3 // 4)
    early = [k for k in range(split) if k != far]
    late = list(range(split, devices))
    returned = {}
    *results, down = experts([arrived[k] for k in [far] + early], gate_up, down, True)
    for k, result in zip([far] + early, results):
        returned[k] = send_back(result, k)
    results = experts([arrived[k] for k in late], gate_up, down, False)
    for k, result in zip(late, results):
        returned[k] = send_back(result, k)
    out = combine(packed, [returned[k] for k in range(devices)])
    return out[None]


def solution(mesh):
    return jax.shard_map(
        shards,
        mesh=mesh,
        in_specs=(
            P("pp", ("grp", "ep"), None),
            P("pp", None),
            P("pp", ("grp", "ep"), None),
            P("pp", ("grp", "ep"), None),
            P("pp", "ep", None, None),
            P("pp", "ep", None, None),
            P(("grp", "ep"), None),
        ),
        out_specs=P("pp", ("grp", "ep"), None),
        check_vma=False,
    )
```

time: 56.1 us -> 45.4 us (0.81)
  local copies, waits for them, and re-layouts: 11 us -> 0 us
  Pallas kernels: 12.9 us -> 21 us
  starting transfers between devices: 16 us -> 11.7 us
  waiting for transfers between devices: 15.6 us -> 12.2 us
    unnamed x16 -> x0, local copies, waits for them, and re-layouts: 11 us -> none
    pallas_call x1 -> x3, Pallas kernels: 1.57 us -> 9.3 us  [the longest x1 5.32 us: load(): pl.pallas_call(functools.partial(load_kernel, parts), out_shape=pltpu.VME...]
    ppermute x4, starting transfers between devices: 10.7 us -> 6.23 us  [send_back(): lax.ppermute(value, ('ep', 'pp'), [(offset_target(i, offset, devices) * s...]
    ppermute x3, waiting for transfers between devices: 4.69 us -> 1.27 us  [dispatch(): lax.ppermute(value, 'ep', [(i, offset_target(i, offset, devices)) for i i...]
    ppermute x2 -> x1, starting transfers between devices: 2.64 us -> 2.67 us  [onward(): lax.ppermute(value, 'pp', [(i, (i + 1) % sections) for i in range(section...]
  transfers between devices with their start and end apart: 9 -> 8, of which waited for: 4 -> 4; matrix products, arithmetic and copies ran while one was open for 0% -> 0% of each run, Pallas kernels for 17% -> 38%
where the time goes in v2:
time: 45.4 us; the launch traced here: 45 us
  Pallas kernels  21 us (46%)
  waiting for transfers between devices  12.2 us (27%)
  starting transfers between devices  11.7 us (26%)
    ppermute x4, waiting for transfers between devices, send_back(): lax.ppermute(value, ('ep', 'pp'), [(offset_target(i, offset, devices) * s...  11 us
    pallas_call x2, Pallas kernels, experts(): pl.pallas_call(functools.partial(expert_kernel, count, chunk_of(width, 51...  9.83 us
    ppermute x4, starting transfers between devices, send_back(): lax.ppermute(value, ('ep', 'pp'), [(offset_target(i, offset, devices) * s...  6.23 us
    pallas_call x1, Pallas kernels, load(): pl.pallas_call(functools.partial(load_kernel, parts), out_shape=pltpu.VME...  5.32 us
    ppermute x3, starting transfers between devices, dispatch(): lax.ppermute(value, 'ep', [(i, offset_target(i, offset, devices)) for i i...  2.78 us
    ppermute x1, starting transfers between devices, onward(): lax.ppermute(value, 'pp', [(i, (i + 1) % sections) for i in range(section...  2.67 us
    pallas_call x1, Pallas kernels, route_rest(): pl.pallas_call(functools.partial(rest_kernel, devices, offsets), out_shap...  2.1 us
    pallas_call x1, Pallas kernels, route_first(): pl.pallas_call(functools.partial(first_kernel, devices, offset), out_shap...  1.89 us
  transfers between devices with their start and end apart: 8, of which 4 were waited for; matrix products, arithmetic and copies ran while one was open for 0% of the time, Pallas kernels for 38%

profile of v2, /device:TPU:9, one launch (start us, length us, event | category | flops | bytes accessed | tf_op | source)
XLA Modules:
  0.0 45.0 jit_solution(6301676265830876266)
XLA Ops:
  0.0 0.1 pad_add_fusion.place
  0.1 1.9 %shard_map.73 = (bf16[24,3584]{1,0:T(8,128)(2,1)S(1)}, bf16[32,3584]{1,0:T(8,128)(2,1)S(1)}) custom-call(s32[2]{0:T(128)S(1)} %pad_add_fusion.place, bf16[32,3584]{1,0:T(8,128)(2,1)} %bitcast.14, bf16[1,3584]{1,0:T(2,128)(2,1)} %gain_at.1, s32[2,32]{1,0:T(2,128)} %bitcast.16), custom_call_target="tpu_custom_call" | custom-call | tf_op jit(solution)/shard_map/pallas_call | solution.py:90
  2.0 2.4 %collective-permute-start.1 = (bf16[24,3584]{1,0:T(8,128)(2,1)S(1)}, bf16[24,3584]{1,0:T(8,128)(2,1)S(1)}, u32[]{:S(2)}, u32[]{:S(2)}) collective-permute-start(bf16[24,3584]{1,0:T(8,128)(2,1)S(1)} %get-tuple-element.20), channel_id=1, source_target_pairs={{0,8},{4,12},{8,0},{12,4},{1,9},{5,13},{9,1},{13,5},{2,10},{6,14},... | collective-permute-start | bytes 516104 | tf_op jit(solution)/shard_map/ppermute | solution.py:313
  4.3 2.1 %shard_map.74 = (bf16[24,3584]{1,0:T(8,128)(2,1)S(1)}, bf16[24,3584]{1,0:T(8,128)(2,1)S(1)}, bf16[24,3584]{1,0:T(8,128)(2,1)S(1)}, bf16[32,3840]{1,0:T(8,128)(2,1)S(1)}) custom-call(s32[2]{0:T(128)S(1)} %pad_add_fusion.place, bf16[32,3584]{1,0:T(8,128)(2,1)S(1)} %get-tuple-element.17.normed, bf16[32,3584]{1,0:T(8,128)(2,1)} %bitcast.15, s32[2,32]{1,0:T(2,128)} %bitcast.17, ...), custom_call_target="tpu_custom_call" | custom-call | tf_op jit(solution)/shard_map/pallas_call | solution.py:166
  6.5 0.2 collective-permute-start.2
  6.7 0.2 collective-permute-start.6
  6.9 5.3 %shard_map.75.refs_3_.refs_1_ = bf16[3584,2048]{1,0:T(8,128)(2,1)S(1)} custom-call(bf16[3584,2048]{1,0:T(8,128)(2,1)} %bitcast.12), custom_call_target="tpu_custom_call" | custom-call | bytes 14680064 | tf_op jit(solution)/shard_map/pallas_call | solution.py:192
  12.2 2.7 %collective-permute-start = (bf16[32,3840]{1,0:T(8,128)(2,1)S(1)}, bf16[32,3840]{1,0:T(8,128)(2,1)S(1)}, u32[]{:S(2)}, u32[]{:S(2)}) collective-permute-start(bf16[32,3840]{1,0:T(8,128)(2,1)S(1)} %get-tuple-element.19), channel_id=1, source_target_pairs={{0,1},{1,2},{2,3},{3,0},{4,5},{5,6},{6,7},{7,4},{8,9},{9,10},{10,1... | collective-permute-start | bytes 737288 | tf_op jit(solution)/shard_map/ppermute | solution.py:308
  14.9 0.0 collective-permute-done.1.refs_0_
  14.9 1.3 %collective-permute-done.2.refs_2_ = bf16[24,3584]{1,0:T(8,128)(2,1)S(1)} collective-permute-done((bf16[24,3584]{1,0:T(8,128)(2,1)S(1)}, bf16[24,3584]{1,0:T(8,128)(2,1)S(1)}, u32[]{:S(2)}, u32[]{:S(2)}) %collective-permute-start.2) | collective-permute-done | bytes 172064 | tf_op jit(solution)/shard_map/ppermute | solution.py:313
  16.1 5.2 %shard_map.76 = (bf16[24,3584]{1,0:T(8,128)(2,1)S(1)}, bf16[24,3584]{1,0:T(8,128)(2,1)S(1)}, bf16[24,3584]{1,0:T(8,128)(2,1)S(1)}, bf16[1024,3584]{1,0:T(8,128)(2,1)S(1)}) custom-call(bf16[24,3584]{1,0:T(8,128)(2,1)S(1)} %collective-permute-done.1.refs_0_, bf16[24,3584]{1,0:T(8,128)(2,1)S(1)} %get-tuple-element.21.refs_1_, ...), custom_call_target="tpu_custom_call" | custom-call | flops 1585446912 | bytes 22020096 | tf_op jit(solution)/shard_map/pallas_call | solution.py:237
  21.3 2.6 %collective-permute-start.3 = (bf16[24,3584]{1,0:T(8,128)(2,1)S(1)}, bf16[24,3584]{1,0:T(8,128)(2,1)S(1)}, u32[]{:S(2)}, u32[]{:S(2)}) collective-permute-start(bf16[24,3584]{1,0:T(8,128)(2,1)S(1)} %get-tuple-element.24), channel_id=1, source_target_pairs={{0,1},{1,2},{2,3},{3,0},{4,5},{5,6},{6,7},{7,4},{8,9},{9,10},{10,1... | collective-permute-start | bytes 516104 | tf_op jit(solution)/shard_map/ppermute | solution.py:318
  23.9 2.0 %collective-permute-start.4 = (bf16[24,3584]{1,0:T(8,128)(2,1)S(1)}, bf16[24,3584]{1,0:T(8,128)(2,1)S(1)}, u32[]{:S(2)}, u32[]{:S(2)}) collective-permute-start(bf16[24,3584]{1,0:T(8,128)(2,1)S(1)} %get-tuple-element.25), channel_id=1, source_target_pairs={{4,1},{5,2},{6,3},{7,0},{0,5},{1,6},{2,7},{3,4},{12,9},{13,10},{14... | collective-permute-start | bytes 516104 | tf_op jit(solution)/shard_map/ppermute | solution.py:318
  25.9 1.0 %collective-permute-start.5 = (bf16[24,3584]{1,0:T(8,128)(2,1)S(1)}, bf16[24,3584]{1,0:T(8,128)(2,1)S(1)}, u32[]{:S(2)}, u32[]{:S(2)}) collective-permute-start(bf16[24,3584]{1,0:T(8,128)(2,1)S(1)} %get-tuple-element.26), channel_id=1, source_target_pairs={{8,1},{9,2},{10,3},{11,0},{12,5},{13,6},{14,7},{15,4},{0,9},{1,10}... | collective-permute-start | bytes 516104 | tf_op jit(solution)/shard_map/ppermute | solution.py:318
  26.9 0.0 collective-permute-done.6.refs_0_
  26.9 4.6 %shard_map.77 = bf16[24,3584]{1,0:T(8,128)(2,1)S(1)} custom-call(bf16[24,3584]{1,0:T(8,128)(2,1)S(1)} %collective-permute-done.6.refs_0_, bf16[3584,2048]{1,0:T(8,128)(2,1)S(1)} %shard_map.75.refs_3_.refs_1_, bf16[1024,3584]{1,0:T(8,128)(2,1)S(1)} %get-tuple-element.28.refs_2_), custom_call_target="tpu_custom_call" | custom-call | flops 528482304 | bytes 22020096 | tf_op jit(solution)/shard_map/pallas_call | solution.py:237
  31.5 0.7 %collective-permute-start.7 = (bf16[24,3584]{1,0:T(8,128)(2,1)S(1)}, bf16[24,3584]{1,0:T(8,128)(2,1)S(1)}, u32[]{:S(2)}, u32[]{:S(2)}) collective-permute-start(bf16[24,3584]{1,0:T(8,128)(2,1)S(1)} %shard_map.77), channel_id=1, source_target_pairs={{12,1},{13,2},{14,3},{15,0},{8,5},{9,6},{10,7},{11,4},{4,9},{5,10}... | collective-permute-start | bytes 516104 | tf_op jit(solution)/shard_map/ppermute | solution.py:318
  32.2 0.0 collective-permute-done.packed
  32.2 0.0 collective-permute-done.3.refs_0_
  32.2 0.6 %collective-permute-done.4.refs_1_ = bf16[24,3584]{1,0:T(8,128)(2,1)S(1)} collective-permute-done((bf16[24,3584]{1,0:T(8,128)(2,1)S(1)}, bf16[24,3584]{1,0:T(8,128)(2,1)S(1)}, u32[]{:S(2)}, u32[]{:S(2)}) %collective-permute-start.4) | collective-permute-done | bytes 172064 | tf_op jit(solution)/shard_map/ppermute | solution.py:318
  32.8 2.6 %collective-permute-done.5.refs_2_ = bf16[24,3584]{1,0:T(8,128)(2,1)S(1)} collective-permute-done((bf16[24,3584]{1,0:T(8,128)(2,1)S(1)}, bf16[24,3584]{1,0:T(8,128)(2,1)S(1)}, u32[]{:S(2)}, u32[]{:S(2)}) %collective-permute-start.5) | collective-permute-done | bytes 172064 | tf_op jit(solution)/shard_map/ppermute | solution.py:318
  35.4 7.8 %collective-permute-done.7.refs_3_ = bf16[24,3584]{1,0:T(8,128)(2,1)S(1)} collective-permute-done((bf16[24,3584]{1,0:T(8,128)(2,1)S(1)}, bf16[24,3584]{1,0:T(8,128)(2,1)S(1)}, u32[]{:S(2)}, u32[]{:S(2)}) %collective-permute-start.7) | collective-permute-done | bytes 172064 | tf_op jit(solution)/shard_map/ppermute | solution.py:318
  43.2 1.9 %shard_map.78 = bf16[32,3584]{1,0:T(8,128)(2,1)} custom-call(bf16[32,3840]{1,0:T(8,128)(2,1)S(1)} %collective-permute-done.packed, bf16[24,3584]{1,0:T(8,128)(2,1)S(1)} %collective-permute-done.3.refs_0_, bf16[24,3584]{1,0:T(8,128)(2,1)S(1)} %collective-permute-done.4.refs_1_, bf16[24,3584]{1,0:T(8,128)(2,1)S(1)} %collective-permute-done.5.refs_2_, ...), custom_call_target="tpu_custom_call" | custom-call | tf_op jit(solution)/shard_map/pallas_call | solution.py:278
Async XLA Ops:
  2.0 12.9 %collective-permute-start.1 = (bf16[24,3584]{1,0:T(8,128)(2,1)S(1)}, bf16[24,3584]{1,0:T(8,128)(2,1)S(1)}, u32[]{:S(2)}, u32[]{:S(2)}) collective-permute-start(bf16[24,3584]{1,0:T(8,128)(2,1)S(1)} %get-tuple-element.20), channel_id=1, source_target_pairs={{0,8},{4,12},{8,0},{12,4},{1,9},{5,13},{9,1},{13,5},{2,10},{6,14},... | collective-permute-start | bytes 516104 | tf_op jit(solution)/shard_map/ppermute | solution.py:313
  6.5 9.7 %collective-permute-start.2 = (bf16[24,3584]{1,0:T(8,128)(2,1)S(1)}, bf16[24,3584]{1,0:T(8,128)(2,1)S(1)}, u32[]{:S(2)}, u32[]{:S(2)}) collective-permute-start(bf16[24,3584]{1,0:T(8,128)(2,1)S(1)} %get-tuple-element.22), channel_id=1, source_target_pairs={{0,4},{4,0},{8,12},{12,8},{1,5},{5,1},{9,13},{13,9},{2,6},{6,2},{1... | collective-permute-start | bytes 516104 | tf_op jit(solution)/shard_map/ppermute | solution.py:313
  6.7 20.2 %collective-permute-start.6 = (bf16[24,3584]{1,0:T(8,128)(2,1)S(1)}, bf16[24,3584]{1,0:T(8,128)(2,1)S(1)}, u32[]{:S(2)}, u32[]{:S(2)}) collective-permute-start(bf16[24,3584]{1,0:T(8,128)(2,1)S(1)} %get-tuple-element.27), channel_id=1, source_target_pairs={{0,12},{4,8},{8,4},{12,0},{1,13},{5,9},{9,5},{13,1},{2,14},{6,10},... | collective-permute-start | bytes 516104 | tf_op jit(solution)/shard_map/ppermute | solution.py:313
  12.2 20.0 %collective-permute-start = (bf16[32,3840]{1,0:T(8,128)(2,1)S(1)}, bf16[32,3840]{1,0:T(8,128)(2,1)S(1)}, u32[]{:S(2)}, u32[]{:S(2)}) collective-permute-start(bf16[32,3840]{1,0:T(8,128)(2,1)S(1)} %get-tuple-element.19), channel_id=1, source_target_pairs={{0,1},{1,2},{2,3},{3,0},{4,5},{5,6},{6,7},{7,4},{8,9},{9,10},{10,1... | collective-permute-start | bytes 737288 | tf_op jit(solution)/shard_map/ppermute | solution.py:308
  21.3 10.9 %collective-permute-start.3 = (bf16[24,3584]{1,0:T(8,128)(2,1)S(1)}, bf16[24,3584]{1,0:T(8,128)(2,1)S(1)}, u32[]{:S(2)}, u32[]{:S(2)}) collective-permute-start(bf16[24,3584]{1,0:T(8,128)(2,1)S(1)} %get-tuple-element.24), channel_id=1, source_target_pairs={{0,1},{1,2},{2,3},{3,0},{4,5},{5,6},{6,7},{7,4},{8,9},{9,10},{10,1... | collective-permute-start | bytes 516104 | tf_op jit(solution)/shard_map/ppermute | solution.py:318
  23.9 8.9 %collective-permute-start.4 = (bf16[24,3584]{1,0:T(8,128)(2,1)S(1)}, bf16[24,3584]{1,0:T(8,128)(2,1)S(1)}, u32[]{:S(2)}, u32[]{:S(2)}) collective-permute-start(bf16[24,3584]{1,0:T(8,128)(2,1)S(1)} %get-tuple-element.25), channel_id=1, source_target_pairs={{4,1},{5,2},{6,3},{7,0},{0,5},{1,6},{2,7},{3,4},{12,9},{13,10},{14... | collective-permute-start | bytes 516104 | tf_op jit(solution)/shard_map/ppermute | solution.py:318
  25.9 9.5 %collective-permute-start.5 = (bf16[24,3584]{1,0:T(8,128)(2,1)S(1)}, bf16[24,3584]{1,0:T(8,128)(2,1)S(1)}, u32[]{:S(2)}, u32[]{:S(2)}) collective-permute-start(bf16[24,3584]{1,0:T(8,128)(2,1)S(1)} %get-tuple-element.26), channel_id=1, source_target_pairs={{8,1},{9,2},{10,3},{11,0},{12,5},{13,6},{14,7},{15,4},{0,9},{1,10}... | collective-permute-start | bytes 516104 | tf_op jit(solution)/shard_map/ppermute | solution.py:318
  31.5 11.7 %collective-permute-start.7 = (bf16[24,3584]{1,0:T(8,128)(2,1)S(1)}, bf16[24,3584]{1,0:T(8,128)(2,1)S(1)}, u32[]{:S(2)}, u32[]{:S(2)}) collective-permute-start(bf16[24,3584]{1,0:T(8,128)(2,1)S(1)} %shard_map.77), channel_id=1, source_target_pairs={{12,1},{13,2},{14,3},{15,0},{8,5},{9,6},{10,7},{11,4},{4,9},{5,10}... | collective-permute-start | bytes 516104 | tf_op jit(solution)/shard_map/ppermute | solution.py:318

commit v3 on v2

v3 whole, which is shorter than its diff:
```python
import functools

import jax
import jax.numpy as jnp
from jax import lax
from jax.experimental import pallas as pl
from jax.experimental.pallas import tpu as pltpu
from jax.sharding import PartitionSpec as P

EXPERTS = 4
TOP = 2
CAP = 24
OWN = 32
AHEAD = 8

guidance_scale = 2.5
epsilon = 1e-06
F32 = jnp.float32
BF16 = jnp.bfloat16
VMEM = pl.BlockSpec(memory_space=pltpu.VMEM)
SMEM = pl.BlockSpec(memory_space=pltpu.SMEM)
HBM = pl.BlockSpec(memory_space=pltpu.HBM)


def chunk_of(extent, largest):
    size = largest
    while extent % size:
        size //= 2
    return size


def in_hbm(*arrays):
    return [pltpu.with_memory_space_constraint(a, pltpu.HBM) for a in arrays]


def lanes_for(extent):
    return -(-extent // 128) * 128


def offset_target(me, offset, devices):
    if devices & (devices - 1) == 0:
        return me ^ offset
    return (me + offset) % devices


def fetch(pairs, sems, others=()):
    copies = [pltpu.make_async_copy(s, d, sems.at[i]) for i, (s, d) in enumerate(pairs)]
    for copy in [*copies, *others]:
        copy.start()
    for copy in copies:
        copy.wait()


def slot_positions(ids, rows):
    line = lax.broadcasted_iota(jnp.int32, (rows, rows), 0)
    lane = lax.broadcasted_iota(jnp.int32, (rows, rows), 1)
    expert = lax.broadcasted_iota(jnp.int32, (EXPERTS, rows), 0)
    named = jnp.zeros((EXPERTS, rows), F32)
    for k in range(TOP):
        named = named + (ids[k : k + 1, :] == expert).astype(F32)
    position = jnp.dot(named, (line < lane).astype(F32), preferred_element_type=F32)
    return jnp.where(named > 0.0, position, -1.0)


def of_expert(table, own):
    expert = lax.broadcasted_iota(jnp.int32, table.shape, 0)
    return jnp.sum(jnp.where(expert == own, table, 0.0), axis=0, keepdims=True)


def choice_of(position, own, rows):
    slot = lax.broadcasted_iota(jnp.int32, (CAP, rows), 0).astype(F32)
    return (of_expert(position, own) == slot).astype(F32)


def pick(choice, normed):
    return jnp.dot(choice.astype(BF16), normed, preferred_element_type=F32).astype(BF16)


def first_kernel(devices, offsets, place, hidden_at, gain_at, ids_at, *refs):
    picked, (normed, hidden, gain, ids, sems) = refs[: len(offsets)], refs[len(offsets) :]
    pairs = [(ids_at, ids), (hidden_at, hidden), (gain_at, gain)]
    copies = [pltpu.make_async_copy(s, d, sems.at[i]) for i, (s, d) in enumerate(pairs)]
    for copy in copies:
        copy.start()
    rows, _ = hidden.shape
    copies[0].wait()
    position = slot_positions(ids, rows)
    owners = [offset_target(place[0], k, devices) // (devices // EXPERTS) for k in offsets]
    choices = [choice_of(position, own, rows) for own in owners]
    copies[1].wait()
    copies[2].wait()
    widened = hidden[...].astype(F32)
    factor = lax.rsqrt(jnp.mean(widened * widened, axis=-1, keepdims=True) + epsilon)
    normed[...] = (widened * factor * gain[...].astype(F32)).astype(BF16)
    for ref, choice in zip(picked, choices):
        ref[...] = pick(choice, normed[...])


def route_first(place, hidden, gain, ids, devices, offsets):
    rows, width = hidden.shape
    return pl.pallas_call(
        functools.partial(first_kernel, devices, offsets),
        out_shape=[jax.ShapeDtypeStruct((CAP, width), BF16)] * len(offsets)
        + [jax.ShapeDtypeStruct((rows, width), BF16)],
        in_specs=[SMEM] + [HBM] * 3,
        out_specs=[VMEM] * (len(offsets) + 1),
        scratch_shapes=[
            pltpu.VMEM(hidden.shape, BF16),
            pltpu.VMEM(gain.shape, BF16),
            pltpu.VMEM(ids.shape, jnp.int32),
            pltpu.SemaphoreType.DMA((3,)),
        ],
        compiler_params=pltpu.CompilerParams(vmem_limit_bytes=8 << 20),
    )(place, *in_hbm(hidden, gain, ids))


def rest_kernel(
    devices, offsets, parts, place, normed, hidden_at, ids_at, gates_at, partner_at, weights_at, *refs
):
    picked, (packed, weights) = refs[: len(offsets)], refs[len(offsets) : len(offsets) + 2]
    ids, gates, partner, sems, weight_sems = refs[len(offsets) + 2 :]
    rows, width = normed.shape
    size = weights.shape[0] // parts
    copies = [
        pltpu.make_async_copy(
            weights_at.at[pl.ds(i * size, size)], weights.at[pl.ds(i * size, size)], weight_sems.at[i]
        )
        for i in range(parts)
    ]
    fetch(
        [
            (ids_at, ids),
            (gates_at, gates),
            (partner_at, partner),
            (hidden_at, packed.at[pl.ds(0, rows), pl.ds(0, width)]),
        ],
        sems,
        copies,
    )
    middle = rows // 2
    me, is_last = place[0], place[1]
    position = slot_positions(ids, rows)
    expert = lax.broadcasted_iota(jnp.int32, (EXPERTS, rows), 0)
    weight = jnp.zeros((EXPERTS, rows), F32)
    for k in range(TOP):
        weight = weight + jnp.where(ids[k : k + 1, :] == expert, gates[k : k + 1, :], 0.0)

    line = lax.broadcasted_iota(jnp.int32, (rows, rows), 0)
    lane = lax.broadcasted_iota(jnp.int32, (rows, rows), 1)
    same_row = (line == lane).astype(F32)
    weighted = [same_row]
    for offset in range(devices):
        own = offset_target(me, offset, devices) // (devices // EXPERTS)
        choice = choice_of(position, own, rows)
        weighted.append(choice * of_expert(weight, own))
        if offset in offsets:
            picked[offsets.index(offset)][...] = pick(choice, normed[...])

    pair_line = lax.broadcasted_iota(jnp.int32, (rows, middle), 0)
    pair_lane = lax.broadcasted_iota(jnp.int32, (rows, middle), 1)
    pair = jnp.sum(
        jnp.where(pair_line == pair_lane, partner[...].astype(F32), 0.0), axis=1, keepdims=True
    )
    weak_row = (lane.astype(F32) == pair + float(middle)).astype(F32)
    guided = guidance_scale * same_row + (1.0 - guidance_scale) * weak_row
    guide = jnp.where(jnp.logical_and(line < middle, is_last > 0), guided, same_row)
    span = (packed.shape[1] - width) // 2
    if span > rows + devices * CAP:
        weighted.append(jnp.zeros((span - rows - devices * CAP, rows), F32))
    mix = lax.dot_general(
        guide,
        jnp.concatenate(weighted, axis=0),
        (((1,), (1,)), ((), ())),
        precision=lax.Precision.HIGHEST,
        preferred_element_type=F32,
    )
    high = mix.astype(BF16)
    packed[:rows, width : width + span] = high
    packed[:rows, width + span :] = (mix - high.astype(F32)).astype(BF16)
    packed[rows:, :] = jnp.zeros((OWN, packed.shape[1]), BF16)
    for copy in copies:
        copy.wait()


def route_rest(place, normed, hidden, ids, gates, partner, weights, devices, offsets):
    parts = 7 if weights.shape[0] % 112 == 0 else 1
    rows, width = normed.shape
    span = lanes_for(rows + devices * CAP)
    return pl.pallas_call(
        functools.partial(rest_kernel, devices, offsets, parts),
        out_shape=[jax.ShapeDtypeStruct((CAP, width), BF16)] * len(offsets)
        + [jax.ShapeDtypeStruct((rows + OWN, width + 2 * span), BF16)]
        + [pltpu.VMEM(weights.shape, weights.dtype)],
        in_specs=[SMEM, VMEM] + [HBM] * 5,
        out_specs=[VMEM] * (len(offsets) + 2),
        scratch_shapes=[
            pltpu.VMEM(ids.shape, jnp.int32),
            pltpu.VMEM(gates.shape, F32),
            pltpu.VMEM(partner.shape, jnp.int32),
            pltpu.SemaphoreType.DMA((4,)),
            pltpu.SemaphoreType.DMA((parts,)),
        ],
        compiler_params=pltpu.CompilerParams(vmem_limit_bytes=8 << 20),
        cost_estimate=pl.CostEstimate(
            flops=0, bytes_accessed=2 * weights.size, transcendentals=0
        ),
    )(place, normed, *in_hbm(hidden, ids, gates, partner, weights))


def hidden_units(rows, weights):
    stacked = jnp.concatenate([r[...].astype(F32) for r in rows], axis=0).astype(BF16)
    projected = jnp.dot(stacked, weights[...], preferred_element_type=F32)
    half = projected.shape[1] // 2
    gate, up = projected[:, :half], projected[:, half:]
    return (gate / (1.0 + jnp.exp(-gate)) * up).astype(BF16)


def early_kernel(count, step, *refs):
    rows, (packed_in, gate_up, down_at) = refs[:count], refs[count : count + 3]
    outs, (packed, down, down_sem) = refs[count + 3 : 2 * count + 2], refs[2 * count + 2 :]
    copy = pltpu.make_async_copy(down_at, down, down_sem)
    copy.start()
    active = hidden_units(rows, gate_up)
    own_at = packed.shape[0] - OWN
    copy.wait()
    for i in range(down.shape[1] // step):
        at = pl.ds(i * step, step)
        part = jnp.dot(active, down[:, at], preferred_element_type=F32)
        for k in range(count - 1):
            outs[k][:, at] = part[k * CAP : (k + 1) * CAP].astype(BF16)
        own = jnp.concatenate([part[(count - 1) * CAP :], jnp.zeros((OWN - CAP, step), F32)], axis=0)
        packed[own_at:, at] = own.astype(BF16)


def early_experts(rows, packed, gate_up, down):
    count = len(rows)
    width = down.shape[1]
    total = count * CAP
    *results, packed, down = pl.pallas_call(
        functools.partial(early_kernel, count, chunk_of(width, 512)),
        out_shape=[jax.ShapeDtypeStruct((CAP, width), BF16)] * (count - 1)
        + [jax.ShapeDtypeStruct(packed.shape, BF16), pltpu.VMEM(down.shape, down.dtype)],
        in_specs=[VMEM] * (count + 2) + [HBM],
        out_specs=[VMEM] * (count + 1),
        input_output_aliases={count: count - 1},
        scratch_shapes=[pltpu.SemaphoreType.DMA],
        compiler_params=pltpu.CompilerParams(vmem_limit_bytes=(6 << 20) + total * width * 8),
        cost_estimate=pl.CostEstimate(
            flops=2 * total * (gate_up.size + down.size),
            bytes_accessed=2 * (gate_up.size + down.size),
            transcendentals=total * down.shape[0],
        ),
    )(*rows, packed, gate_up, *in_hbm(down))
    return results, packed, down


def late_kernel(count, step, *refs):
    rows, (gate_up, down), outs = refs[:count], refs[count : count + 2], refs[count + 2 :]
    active = hidden_units(rows, gate_up)
    for i in range(down.shape[1] // step):
        at = pl.ds(i * step, step)
        part = jnp.dot(active, down[:, at], preferred_element_type=F32)
        for k in range(count):
            outs[k][:, at] = part[k * CAP : (k + 1) * CAP].astype(BF16)


def late_experts(rows, gate_up, down):
    count = len(rows)
    width = down.shape[1]
    total = count * CAP
    return pl.pallas_call(
        functools.partial(late_kernel, count, chunk_of(width, 512)),
        out_shape=[jax.ShapeDtypeStruct((CAP, width), BF16)] * count,
        in_specs=[VMEM] * (count + 2),
        out_specs=[VMEM] * count,
        compiler_params=pltpu.CompilerParams(vmem_limit_bytes=(6 << 20) + total * width * 8),
        cost_estimate=pl.CostEstimate(
            flops=2 * AHEAD * total * (gate_up.size + down.size),
            bytes_accessed=2 * AHEAD * (gate_up.size + down.size),
            transcendentals=total * down.shape[0],
        ),
    )(*rows, gate_up, down)


def combine_kernel(count, step, packed, *refs):
    slots, out_at, out, sems = refs[:count], *refs[count:]
    rows, width = out.shape
    span = (packed.shape[1] - width) // 2
    used = rows + (count + 1) * CAP
    high = packed[:rows, width : width + span][:, :used]
    low = packed[:rows, width + span :][:, :used]

    def copy(i):
        at = pl.ds(i * step, step)
        return pltpu.make_async_copy(out.at[:, at], out_at.at[:, at], sems.at[i])

    for i in range(width // step):
        at = pl.ds(i * step, step)
        stacked = jnp.concatenate(
            [packed[:rows, at].astype(F32), packed[rows:, at].astype(F32)[:CAP]]
            + [s[:, at].astype(F32) for s in slots],
            axis=0,
        ).astype(BF16)
        out[:, at] = (
            jnp.dot(high, stacked, preferred_element_type=F32)
            + jnp.dot(low, stacked, preferred_element_type=F32)
        ).astype(BF16)
        copy(i).start()
    for i in range(width // step):
        copy(i).wait()


def combine(packed, slots):
    count = len(slots)
    rows, width = packed.shape[0] - OWN, slots[0].shape[1]
    step = chunk_of(width, 512)
    return pl.pallas_call(
        functools.partial(combine_kernel, count, step),
        out_shape=jax.ShapeDtypeStruct((rows, width), BF16),
        in_specs=[VMEM] * (count + 1),
        out_specs=HBM,
        scratch_shapes=[
            pltpu.VMEM((rows, width), BF16),
            pltpu.SemaphoreType.DMA((width // step,)),
        ],
        compiler_params=pltpu.CompilerParams(vmem_limit_bytes=8 << 20),
    )(packed, *slots)


def shards(hidden, norm_gain, expert_ids, gate_weights, expert_gate_up, expert_down, partner):
    devices = lax.axis_size("ep")
    sections = lax.axis_size("pp")
    place = jnp.stack(
        [lax.axis_index("ep"), (lax.axis_index("pp") == sections - 1).astype(jnp.int32)]
    )
    section_rows = hidden[0]
    gate_up = expert_gate_up[0, 0]
    down = expert_down[0, 0]

    far, split = devices // 2, max(1, devices * 3 // 4)
    early = [far] + [k for k in range(1, split) if k != far]
    late = list(range(split, devices))
    ids, gates = expert_ids[0].T, gate_weights[0].T
    *picked, normed = route_first(place, section_rows, norm_gain, ids, devices, early)
    *rest, packed, gate_up = route_rest(
        place, normed, section_rows, ids, gates, partner, gate_up, devices, late + [0]
    )
    picked = dict(zip(early + late + [0], picked + rest))

    def onward(value):
        return lax.ppermute(value, "pp", [(i, (i + 1) % sections) for i in range(sections)])

    def dispatch(value, offset):
        if offset == 0:
            return value
        return lax.ppermute(
            value, "ep", [(i, offset_target(i, offset, devices)) for i in range(devices)]
        )

    def send_back(value, offset):
        return lax.ppermute(
            value,
            ("ep", "pp"),
            [
                (offset_target(i, offset, devices) * sections + p, i * sections + (p + 1) % sections)
                for i in range(devices)
                for p in range(sections)
            ],
        )

    arrived = {k: dispatch(picked[k], k) for k in early + late + [0]}
    results, packed, down = early_experts(
        [arrived[k] for k in early + [0]], packed, gate_up, down
    )
    returned = {k: send_back(result, k) for k, result in zip(early, results)}
    packed = onward(packed)
    results = late_experts([arrived[k] for k in late], gate_up, down)
    returned.update({k: send_back(result, k) for k, result in zip(late, results)})
    out = combine(packed, [returned[k] for k in range(1, devices)])
    return out[None]


def solution(mesh):
    return jax.shard_map(
        shards,
        mesh=mesh,
        in_specs=(
            P("pp", ("grp", "ep"), None),
            P("pp", None),
            P("pp", ("grp", "ep"), None),
            P("pp", ("grp", "ep"), None),
            P("pp", "ep", None, None),
            P("pp", "ep", None, None),
            P(("grp", "ep"), None),
        ),
        out_specs=P("pp", ("grp", "ep"), None),
        check_vma=False,
    )
```

time: 45.4 us -> 38.4 us (0.85)
  Pallas kernels: 21 us -> 17.4 us
  starting transfers between devices: 11.7 us -> 9.2 us
  waiting for transfers between devices: 12.2 us -> 11.5 us
    pallas_call x6 -> x5, Pallas kernels: 21 us -> 17.4 us  [the longest x1 6.01 us: route_rest(): pl.pallas_call(functools.partial(rest_kernel, devices, offsets, parts), o...]
    ppermute x1, starting transfers between devices: 2.67 us -> 0.08 us  [onward(): lax.ppermute(value, 'pp', [(i, (i + 1) % sections) for i in range(section...]
    ppermute x4 -> x3, waiting for transfers between devices: 11 us -> 10.3 us  [send_back(): lax.ppermute(value, ('ep', 'pp'), [(offset_target(i, offset, devices) * s...]
    ppermute x4 -> x3, starting transfers between devices: 6.23 us -> 6.32 us  [send_back(): lax.ppermute(value, ('ep', 'pp'), [(offset_target(i, offset, devices) * s...]
  transfers between devices with their start and end apart: 8 -> 7, of which waited for: 4 -> 3; matrix products, arithmetic and copies ran while one was open for 0% -> 0% of each run, Pallas kernels for 38% -> 38%
where the time goes in v3:
time: 38.4 us; the launch traced here: 38.2 us
  Pallas kernels  17.4 us (45%)
  waiting for transfers between devices  11.5 us (30%)
  starting transfers between devices  9.2 us (24%)
    ppermute x3, waiting for transfers between devices, send_back(): lax.ppermute(value, ('ep', 'pp'), [(offset_target(i, offset, devices) * s...  10.3 us
    ppermute x3, starting transfers between devices, send_back(): lax.ppermute(value, ('ep', 'pp'), [(offset_target(i, offset, devices) * s...  6.32 us
    pallas_call x1, Pallas kernels, route_rest(): pl.pallas_call(functools.partial(rest_kernel, devices, offsets, parts), o...  6.01 us
    pallas_call x1, Pallas kernels, early_experts(): pl.pallas_call(functools.partial(early_kernel, count, chunk_of(width, 512...  4.48 us
    pallas_call x1, Pallas kernels, late_experts(): pl.pallas_call(functools.partial(late_kernel, count, chunk_of(width, 512)...  3.89 us
    ppermute x3, starting transfers between devices, dispatch(): lax.ppermute(value, 'ep', [(i, offset_target(i, offset, devices)) for i i...  2.8 us
    pallas_call x1, Pallas kernels, route_first(): pl.pallas_call(functools.partial(first_kernel, devices, offsets), out_sha...  1.93 us
    ppermute x3, waiting for transfers between devices, dispatch(): lax.ppermute(value, 'ep', [(i, offset_target(i, offset, devices)) for i i...  1.23 us
  transfers between devices with their start and end apart: 7, of which 3 were waited for; matrix products, arithmetic and copies ran while one was open for 0% of the time, Pallas kernels for 38%

profile of v3, /device:TPU:9, one launch (start us, length us, event | category | flops | bytes accessed | tf_op | source)
XLA Modules:
  0.0 38.2 jit_solution(17926716614156246057)
XLA Ops:
  0.0 0.1 pad_add_fusion.place
  0.1 1.9 %shard_map.73 = (bf16[24,3584]{1,0:T(8,128)(2,1)S(1)}, bf16[24,3584]{1,0:T(8,128)(2,1)S(1)}, bf16[32,3584]{1,0:T(8,128)(2,1)S(1)}) custom-call(s32[2]{0:T(128)S(1)} %pad_add_fusion.place, bf16[32,3584]{1,0:T(8,128)(2,1)} %bitcast.14, bf16[1,3584]{1,0:T(2,128)(2,1)} %gain_at.1, s32[2,32]{1,0:T(2,128)} %bitcast.16), custom_call_target="tpu_custom_call" | custom-call | tf_op jit(solution)/shard_map/pallas_call | solution.py:101
  2.0 2.4 %collective-permute-start = (bf16[24,3584]{1,0:T(8,128)(2,1)S(1)}, bf16[24,3584]{1,0:T(8,128)(2,1)S(1)}, u32[]{:S(2)}, u32[]{:S(2)}) collective-permute-start(bf16[24,3584]{1,0:T(8,128)(2,1)S(1)} %get-tuple-element.16), channel_id=1, source_target_pairs={{0,8},{4,12},{8,0},{12,4},{1,9},{5,13},{9,1},{13,5},{2,10},{6,14},... | collective-permute-start | bytes 516104 | tf_op jit(solution)/shard_map/ppermute | solution.py:356
  4.4 0.2 collective-permute-start.1
  4.6 6.0 %shard_map.74 = (bf16[24,3584]{1,0:T(8,128)(2,1)S(1)}, bf16[24,3584]{1,0:T(8,128)(2,1)S(1)}, bf16[64,3840]{1,0:T(8,128)(2,1)S(1)}, bf16[3584,2048]{1,0:T(8,128)(2,1)S(1)}) custom-call(s32[2]{0:T(128)S(1)} %pad_add_fusion.place, bf16[32,3584]{1,0:T(8,128)(2,1)S(1)} %get-tuple-element.18.normed, bf16[32,3584]{1,0:T(8,128)(2,1)} %bitcast.15, s32[2,32]{1,0:T(2,128)} %bitcast.17, ...), custom_call_target="tpu_custom_call" | custom-call | bytes 14680064 | tf_op jit(solution)/shard_map/pallas_call | solution.py:189
  10.6 0.3 collective-permute-start.5
  10.8 1.2 %collective-permute-done.refs_0_ = bf16[24,3584]{1,0:T(8,128)(2,1)S(1)} collective-permute-done((bf16[24,3584]{1,0:T(8,128)(2,1)S(1)}, bf16[24,3584]{1,0:T(8,128)(2,1)S(1)}, u32[]{:S(2)}, u32[]{:S(2)}) %collective-permute-start) | collective-permute-done | bytes 172064 | tf_op jit(solution)/shard_map/ppermute | solution.py:356
  12.1 0.0 collective-permute-done.1.refs_1_
  12.1 4.5 %shard_map.75 = (bf16[24,3584]{1,0:T(8,128)(2,1)S(1)}, bf16[24,3584]{1,0:T(8,128)(2,1)S(1)}, bf16[64,3840]{1,0:T(8,128)(2,1)S(1)}, bf16[1024,3584]{1,0:T(8,128)(2,1)S(1)}) custom-call(bf16[24,3584]{1,0:T(8,128)(2,1)S(1)} %collective-permute-done.refs_0_, bf16[24,3584]{1,0:T(8,128)(2,1)S(1)} %collective-permute-done.1.refs_1_, ...), custom_call_target="tpu_custom_call", output_to_operand_aliasing={{2}: (3, {})} | custom-call | flops 1585446912 | bytes 22020096 | tf_op jit(solution)/shard_map/pallas_call | solution.py:239
  16.5 2.7 %collective-permute-start.3 = (bf16[24,3584]{1,0:T(8,128)(2,1)S(1)}, bf16[24,3584]{1,0:T(8,128)(2,1)S(1)}, u32[]{:S(2)}, u32[]{:S(2)}) collective-permute-start(bf16[24,3584]{1,0:T(8,128)(2,1)S(1)} %get-tuple-element.23), channel_id=1, source_target_pairs={{4,1},{5,2},{6,3},{7,0},{0,5},{1,6},{2,7},{3,4},{12,9},{13,10},{14... | collective-permute-start | bytes 516104 | tf_op jit(solution)/shard_map/ppermute | solution.py:361
  19.3 1.9 %collective-permute-start.4 = (bf16[24,3584]{1,0:T(8,128)(2,1)S(1)}, bf16[24,3584]{1,0:T(8,128)(2,1)S(1)}, u32[]{:S(2)}, u32[]{:S(2)}) collective-permute-start(bf16[24,3584]{1,0:T(8,128)(2,1)S(1)} %get-tuple-element.24), channel_id=1, source_target_pairs={{8,1},{9,2},{10,3},{11,0},{12,5},{13,6},{14,7},{15,4},{0,9},{1,10}... | collective-permute-start | bytes 516104 | tf_op jit(solution)/shard_map/ppermute | solution.py:361
  21.2 0.1 collective-permute-start.2
  21.3 0.0 collective-permute-done.5.refs_0_
  21.3 3.9 %shard_map.76 = bf16[24,3584]{1,0:T(8,128)(2,1)S(1)} custom-call(bf16[24,3584]{1,0:T(8,128)(2,1)S(1)} %collective-permute-done.5.refs_0_, bf16[3584,2048]{1,0:T(8,128)(2,1)S(1)} %get-tuple-element.21.refs_4_.refs_1_, bf16[1024,3584]{1,0:T(8,128)(2,1)S(1)} %get-tuple-element.26.refs_2_), custom_call_target="tpu_custom_call" | custom-call | flops 4227858432 | bytes 176160768 | tf_op jit(solution)/shard_map/pallas_call | solution.py:271
  25.1 1.7 %collective-permute-start.6 = (bf16[24,3584]{1,0:T(8,128)(2,1)S(1)}, bf16[24,3584]{1,0:T(8,128)(2,1)S(1)}, u32[]{:S(2)}, u32[]{:S(2)}) collective-permute-start(bf16[24,3584]{1,0:T(8,128)(2,1)S(1)} %shard_map.76), channel_id=1, source_target_pairs={{12,1},{13,2},{14,3},{15,0},{8,5},{9,6},{10,7},{11,4},{4,9},{5,10}... | collective-permute-start | bytes 516104 | tf_op jit(solution)/shard_map/ppermute | solution.py:361
  26.8 0.0 collective-permute-done.3.refs_0_
  26.8 5.9 %collective-permute-done.4.refs_1_ = bf16[24,3584]{1,0:T(8,128)(2,1)S(1)} collective-permute-done((bf16[24,3584]{1,0:T(8,128)(2,1)S(1)}, bf16[24,3584]{1,0:T(8,128)(2,1)S(1)}, u32[]{:S(2)}, u32[]{:S(2)}) %collective-permute-start.4) | collective-permute-done | bytes 172064 | tf_op jit(solution)/shard_map/ppermute | solution.py:361
  32.8 4.3 %collective-permute-done.6.refs_2_ = bf16[24,3584]{1,0:T(8,128)(2,1)S(1)} collective-permute-done((bf16[24,3584]{1,0:T(8,128)(2,1)S(1)}, bf16[24,3584]{1,0:T(8,128)(2,1)S(1)}, u32[]{:S(2)}, u32[]{:S(2)}) %collective-permute-start.6) | collective-permute-done | bytes 172064 | tf_op jit(solution)/shard_map/ppermute | solution.py:361
  37.1 0.0 collective-permute-done.2.packed
  37.1 1.1 %shard_map.77 = bf16[32,3584]{1,0:T(8,128)(2,1)} custom-call(bf16[64,3840]{1,0:T(8,128)(2,1)S(1)} %collective-permute-done.2.packed, bf16[24,3584]{1,0:T(8,128)(2,1)S(1)} %collective-permute-done.3.refs_0_, bf16[24,3584]{1,0:T(8,128)(2,1)S(1)} %collective-permute-done.4.refs_1_, bf16[24,3584]{1,0:T(8,128)(2,1)S(1)} %collective-permute-done.6.refs_2_), custom_call_target="tpu_custom_call" | custom-call | tf_op jit(solution)/shard_map/pallas_call | solution.py:317
Async XLA Ops:
  2.0 10.0 %collective-permute-start = (bf16[24,3584]{1,0:T(8,128)(2,1)S(1)}, bf16[24,3584]{1,0:T(8,128)(2,1)S(1)}, u32[]{:S(2)}, u32[]{:S(2)}) collective-permute-start(bf16[24,3584]{1,0:T(8,128)(2,1)S(1)} %get-tuple-element.16), channel_id=1, source_target_pairs={{0,8},{4,12},{8,0},{12,4},{1,9},{5,13},{9,1},{13,5},{2,10},{6,14},... | collective-permute-start | bytes 516104 | tf_op jit(solution)/shard_map/ppermute | solution.py:356
  4.4 7.7 %collective-permute-start.1 = (bf16[24,3584]{1,0:T(8,128)(2,1)S(1)}, bf16[24,3584]{1,0:T(8,128)(2,1)S(1)}, u32[]{:S(2)}, u32[]{:S(2)}) collective-permute-start(bf16[24,3584]{1,0:T(8,128)(2,1)S(1)} %get-tuple-element.17), channel_id=1, source_target_pairs={{0,4},{4,0},{8,12},{12,8},{1,5},{5,1},{9,13},{13,9},{2,6},{6,2},{1... | collective-permute-start | bytes 516104 | tf_op jit(solution)/shard_map/ppermute | solution.py:356
  10.6 10.7 %collective-permute-start.5 = (bf16[24,3584]{1,0:T(8,128)(2,1)S(1)}, bf16[24,3584]{1,0:T(8,128)(2,1)S(1)}, u32[]{:S(2)}, u32[]{:S(2)}) collective-permute-start(bf16[24,3584]{1,0:T(8,128)(2,1)S(1)} %get-tuple-element.25), channel_id=1, source_target_pairs={{0,12},{4,8},{8,4},{12,0},{1,13},{5,9},{9,5},{13,1},{2,14},{6,10},... | collective-permute-start | bytes 516104 | tf_op jit(solution)/shard_map/ppermute | solution.py:356
  16.5 10.3 %collective-permute-start.3 = (bf16[24,3584]{1,0:T(8,128)(2,1)S(1)}, bf16[24,3584]{1,0:T(8,128)(2,1)S(1)}, u32[]{:S(2)}, u32[]{:S(2)}) collective-permute-start(bf16[24,3584]{1,0:T(8,128)(2,1)S(1)} %get-tuple-element.23), channel_id=1, source_target_pairs={{4,1},{5,2},{6,3},{7,0},{0,5},{1,6},{2,7},{3,4},{12,9},{13,10},{14... | collective-permute-start | bytes 516104 | tf_op jit(solution)/shard_map/ppermute | solution.py:361
  19.3 13.5 %collective-permute-start.4 = (bf16[24,3584]{1,0:T(8,128)(2,1)S(1)}, bf16[24,3584]{1,0:T(8,128)(2,1)S(1)}, u32[]{:S(2)}, u32[]{:S(2)}) collective-permute-start(bf16[24,3584]{1,0:T(8,128)(2,1)S(1)} %get-tuple-element.24), channel_id=1, source_target_pairs={{8,1},{9,2},{10,3},{11,0},{12,5},{13,6},{14,7},{15,4},{0,9},{1,10}... | collective-permute-start | bytes 516104 | tf_op jit(solution)/shard_map/ppermute | solution.py:361
  21.2 16.0 %collective-permute-start.2 = (bf16[64,3840]{1,0:T(8,128)(2,1)S(1)}, bf16[64,3840]{1,0:T(8,128)(2,1)S(1)}, u32[]{:S(2)}, u32[]{:S(2)}) collective-permute-start(bf16[64,3840]{1,0:T(8,128)(2,1)S(1)} %get-tuple-element.22), channel_id=1, source_target_pairs={{0,1},{1,2},{2,3},{3,0},{4,5},{5,6},{6,7},{7,4},{8,9},{9,10},{10,1... | collective-permute-start | bytes 1474568 | tf_op jit(solution)/shard_map/ppermute | solution.py:351
  25.1 12.0 %collective-permute-start.6 = (bf16[24,3584]{1,0:T(8,128)(2,1)S(1)}, bf16[24,3584]{1,0:T(8,128)(2,1)S(1)}, u32[]{:S(2)}, u32[]{:S(2)}) collective-permute-start(bf16[24,3584]{1,0:T(8,128)(2,1)S(1)} %shard_map.76), channel_id=1, source_target_pairs={{12,1},{13,2},{14,3},{15,0},{8,5},{9,6},{10,7},{11,4},{4,9},{5,10}... | collective-permute-start | bytes 516104 | tf_op jit(solution)/shard_map/ppermute | solution.py:361

commit v4 on v3

v4 whole, which is shorter than its diff:
```python
import functools

import jax
import jax.numpy as jnp
from jax import lax
from jax.experimental import pallas as pl
from jax.experimental.pallas import tpu as pltpu
from jax.sharding import PartitionSpec as P

EXPERTS = 4
TOP = 2
CAP = 24
AHEAD = 8

guidance_scale = 2.5
epsilon = 1e-06
F32 = jnp.float32
BF16 = jnp.bfloat16
VMEM = pl.BlockSpec(memory_space=pltpu.VMEM)
HBM = pl.BlockSpec(memory_space=pltpu.HBM)


def chunk_of(extent, largest):
    size = largest
    while extent % size:
        size //= 2
    return size


def in_hbm(*arrays):
    return [pltpu.with_memory_space_constraint(a, pltpu.HBM) for a in arrays]


def lanes_for(extent):
    return -(-extent // 128) * 128


def offset_target(me, offset, devices):
    if devices & (devices - 1) == 0:
        return me ^ offset
    return (me + offset) % devices


def fetch(pairs, sems, others=()):
    copies = [pltpu.make_async_copy(s, d, sems.at[i]) for i, (s, d) in enumerate(pairs)]
    for copy in [*copies, *others]:
        copy.start()
    for copy in copies:
        copy.wait()


def slot_positions(ids, rows):
    line = lax.broadcasted_iota(jnp.int32, (rows, rows), 0)
    lane = lax.broadcasted_iota(jnp.int32, (rows, rows), 1)
    expert = lax.broadcasted_iota(jnp.int32, (EXPERTS, rows), 0)
    named = jnp.zeros((EXPERTS, rows), F32)
    for k in range(TOP):
        named = named + (ids[k : k + 1, :] == expert).astype(F32)
    position = jnp.dot(
        named.astype(BF16), (line < lane).astype(F32).astype(BF16), preferred_element_type=F32
    )
    return jnp.where(named > 0.0, position, -1.0)


def of_expert(table, own):
    expert = lax.broadcasted_iota(jnp.int32, table.shape, 0)
    return jnp.sum(jnp.where(expert == own, table, 0.0), axis=0, keepdims=True)


def choice_of(position, own, rows):
    slot = lax.broadcasted_iota(jnp.int32, (CAP, rows), 0).astype(F32)
    return (of_expert(position, own) == slot).astype(F32)


def pick(choice, rows):
    return jnp.dot(choice.astype(BF16), rows, preferred_element_type=F32).astype(BF16)


def first_kernel(devices, offsets, hidden_at, ids_at, *refs):
    picked, (hidden, ids, sems) = refs[: len(offsets)], refs[len(offsets) :]
    pairs = [(ids_at, ids), (hidden_at, hidden)]
    copies = [pltpu.make_async_copy(s, d, sems.at[i]) for i, (s, d) in enumerate(pairs)]
    for copy in copies:
        copy.start()
    rows, _ = hidden.shape
    copies[0].wait()
    position = slot_positions(ids, rows)
    me = lax.axis_index("ep")
    owners = [offset_target(me, k, devices) // (devices // EXPERTS) for k in offsets]
    choices = jnp.concatenate([choice_of(position, own, rows) for own in owners], axis=0)
    copies[1].wait()
    taken = jnp.dot(choices.astype(BF16), hidden[...], preferred_element_type=F32)
    for k, ref in enumerate(picked):
        ref[...] = taken[k * CAP : (k + 1) * CAP].astype(BF16)


def route_first(hidden, ids, devices, offsets):
    rows, width = hidden.shape
    return pl.pallas_call(
        functools.partial(first_kernel, devices, offsets),
        out_shape=[jax.ShapeDtypeStruct((CAP, width), BF16)] * len(offsets)
        + [pltpu.VMEM((rows, width), BF16)],
        in_specs=[HBM] * 2,
        out_specs=[VMEM] * (len(offsets) + 1),
        scratch_shapes=[pltpu.VMEM(ids.shape, jnp.int32), pltpu.SemaphoreType.DMA((2,))],
        compiler_params=pltpu.CompilerParams(vmem_limit_bytes=8 << 20),
    )(*in_hbm(hidden, ids))


def rest_kernel(
    devices, offsets, order, parts, hidden, ids_at, gates_at, partner_at, gain_at, weights_at, *refs
):
    picked, (packed, gain, weights) = refs[: len(offsets)], refs[len(offsets) : len(offsets) + 3]
    ids, gates, partner, sems, weight_sems = refs[len(offsets) + 3 :]
    rows, width = hidden.shape
    size = weights.shape[0] // parts
    copies = [
        pltpu.make_async_copy(
            weights_at.at[pl.ds(i * size, size)], weights.at[pl.ds(i * size, size)], weight_sems.at[i]
        )
        for i in range(parts)
    ]
    fetch(
        [
            (ids_at, ids),
            (gates_at, gates),
            (partner_at, partner),
            (gain_at, gain),
        ],
        sems,
        copies,
    )
    middle = rows // 2
    me = lax.axis_index("ep")
    is_last = (lax.axis_index("pp") == lax.axis_size("pp") - 1).astype(jnp.int32)
    position = slot_positions(ids, rows)
    expert = lax.broadcasted_iota(jnp.int32, (EXPERTS, rows), 0)
    weight = jnp.zeros((EXPERTS, rows), F32)
    for k in range(TOP):
        weight = weight + jnp.where(ids[k : k + 1, :] == expert, gates[k : k + 1, :], 0.0)

    line = lax.broadcasted_iota(jnp.int32, (rows, rows), 0)
    lane = lax.broadcasted_iota(jnp.int32, (rows, rows), 1)
    same_row = (line == lane).astype(F32)
    weighted = [same_row]
    for offset in order:
        own = offset_target(me, offset, devices) // (devices // EXPERTS)
        choice = choice_of(position, own, rows)
        weighted.append(choice * of_expert(weight, own))
        if offset in offsets:
            picked[offsets.index(offset)][...] = pick(choice, hidden[...])

    pair_line = lax.broadcasted_iota(jnp.int32, (rows, middle), 0)
    pair_lane = lax.broadcasted_iota(jnp.int32, (rows, middle), 1)
    pair = jnp.sum(
        jnp.where(pair_line == pair_lane, partner[...].astype(F32), 0.0), axis=1, keepdims=True
    )
    weak_row = (lane.astype(F32) == pair + float(middle)).astype(F32)
    guided = guidance_scale * same_row + (1.0 - guidance_scale) * weak_row
    guide = jnp.where(jnp.logical_and(line < middle, is_last > 0), guided, same_row)
    span = (packed.shape[1] - width) // 2
    if span > rows + devices * CAP:
        weighted.append(jnp.zeros((span - rows - devices * CAP, rows), F32))
    mix = lax.dot_general(
        guide,
        jnp.concatenate(weighted, axis=0),
        (((1,), (1,)), ((), ())),
        precision=lax.Precision.HIGHEST,
        preferred_element_type=F32,
    )
    high = mix.astype(BF16)
    packed[:, :width] = hidden[...]
    packed[:, width : width + span] = high
    packed[:, width + span :] = (mix - high.astype(F32)).astype(BF16)
    for copy in copies:
        copy.wait()


def route_rest(hidden, ids, gates, partner, gain, weights, devices, offsets, order):
    parts = 7 if weights.shape[0] % 112 == 0 else 1
    rows, width = hidden.shape
    span = lanes_for(rows + devices * CAP)
    return pl.pallas_call(
        functools.partial(rest_kernel, devices, offsets, order, parts),
        out_shape=[jax.ShapeDtypeStruct((CAP, width), BF16)] * len(offsets)
        + [jax.ShapeDtypeStruct((rows, width + 2 * span), BF16)]
        + [pltpu.VMEM(gain.shape, gain.dtype), pltpu.VMEM(weights.shape, weights.dtype)],
        in_specs=[VMEM] + [HBM] * 5,
        out_specs=[VMEM] * (len(offsets) + 3),
        scratch_shapes=[
            pltpu.VMEM(ids.shape, jnp.int32),
            pltpu.VMEM(gates.shape, F32),
            pltpu.VMEM(partner.shape, jnp.int32),
            pltpu.SemaphoreType.DMA((4,)),
            pltpu.SemaphoreType.DMA((parts,)),
        ],
        compiler_params=pltpu.CompilerParams(vmem_limit_bytes=8 << 20),
        cost_estimate=pl.CostEstimate(
            flops=0, bytes_accessed=2 * weights.size, transcendentals=0
        ),
    )(hidden, *in_hbm(ids, gates, partner, gain, weights))


def hidden_units(rows, gain, weights):
    stacked = jnp.concatenate([r[...].astype(F32) for r in rows], axis=0)
    factor = lax.rsqrt(jnp.mean(stacked * stacked, axis=-1, keepdims=True) + epsilon)
    normed = (stacked * factor * gain[...].astype(F32)).astype(BF16)
    projected = jnp.dot(normed, weights[...], preferred_element_type=F32)
    half = projected.shape[1] // 2
    gate, up = projected[:, :half], projected[:, half:]
    return (gate / (1.0 + jnp.exp(-gate)) * up).astype(BF16)


def early_kernel(count, step, *refs):
    rows, (gain, gate_up, down_at) = refs[:count], refs[count : count + 3]
    outs, (down, down_sem) = refs[count + 3 : 2 * count + 3], refs[2 * count + 3 :]
    copy = pltpu.make_async_copy(down_at, down, down_sem)
    copy.start()
    active = hidden_units(rows, gain, gate_up)
    copy.wait()
    for i in range(down.shape[1] // step):
        at = pl.ds(i * step, step)
        part = jnp.dot(active, down[:, at], preferred_element_type=F32)
        for k in range(count):
            outs[k][:, at] = part[k * CAP : (k + 1) * CAP].astype(BF16)


def early_experts(rows, gain, gate_up, down):
    count = len(rows)
    width = down.shape[1]
    total = count * CAP
    *results, down = pl.pallas_call(
        functools.partial(early_kernel, count, chunk_of(width, 512)),
        out_shape=[jax.ShapeDtypeStruct((CAP, width), BF16)] * count
        + [pltpu.VMEM(down.shape, down.dtype)],
        in_specs=[VMEM] * (count + 2) + [HBM],
        out_specs=[VMEM] * (count + 1),
        scratch_shapes=[pltpu.SemaphoreType.DMA],
        compiler_params=pltpu.CompilerParams(vmem_limit_bytes=(6 << 20) + total * width * 8),
        cost_estimate=pl.CostEstimate(
            flops=2 * total * (gate_up.size + down.size),
            bytes_accessed=2 * (gate_up.size + down.size),
            transcendentals=total * down.shape[0],
        ),
    )(*rows, gain, gate_up, *in_hbm(down))
    return results, down


def late_kernel(count, step, *refs):
    rows, (gain, gate_up, down), outs = refs[:count], refs[count : count + 3], refs[count + 3 :]
    active = hidden_units(rows, gain, gate_up)
    for i in range(down.shape[1] // step):
        at = pl.ds(i * step, step)
        part = jnp.dot(active, down[:, at], preferred_element_type=F32)
        for k in range(count):
            outs[k][:, at] = part[k * CAP : (k + 1) * CAP].astype(BF16)


def late_experts(rows, gain, gate_up, down):
    count = len(rows)
    width = down.shape[1]
    total = count * CAP
    return pl.pallas_call(
        functools.partial(late_kernel, count, chunk_of(width, 512)),
        out_shape=[jax.ShapeDtypeStruct((CAP, width), BF16)] * count,
        in_specs=[VMEM] * (count + 3),
        out_specs=[VMEM] * count,
        compiler_params=pltpu.CompilerParams(vmem_limit_bytes=(6 << 20) + total * width * 8),
        cost_estimate=pl.CostEstimate(
            flops=2 * AHEAD * total * (gate_up.size + down.size),
            bytes_accessed=2 * AHEAD * (gate_up.size + down.size),
            transcendentals=total * down.shape[0],
        ),
    )(*rows, gain, gate_up, down)


def mixing(packed, width, at, used):
    span = (packed.shape[1] - width) // 2
    high = packed[:, width : width + span].astype(F32)[:, at : at + used]
    low = packed[:, width + span :].astype(F32)[:, at : at + used]
    return jnp.concatenate([high, low], axis=0).astype(BF16)


def mixed(matrix, stacked):
    both = jnp.dot(matrix, stacked.astype(BF16), preferred_element_type=F32)
    rows = both.shape[0] // 2
    return both[:rows] + both[rows:]


def begin_kernel(count, step, packed, *refs):
    slots, total = refs[:count], refs[count]
    rows, width = total.shape
    matrix = mixing(packed, width, 0, rows + count * CAP)
    for i in range(width // step):
        at = pl.ds(i * step, step)
        stacked = jnp.concatenate(
            [packed[:, at].astype(F32)] + [s[:, at].astype(F32) for s in slots], axis=0
        )
        total[:, at] = mixed(matrix, stacked)


def begin_combine(packed, slots):
    count = len(slots)
    rows, width = packed.shape[0], slots[0].shape[1]
    return pl.pallas_call(
        functools.partial(begin_kernel, count, chunk_of(width, 512)),
        out_shape=jax.ShapeDtypeStruct((rows, width), F32),
        in_specs=[VMEM] * (count + 1),
        out_specs=VMEM,
        compiler_params=pltpu.CompilerParams(vmem_limit_bytes=8 << 20),
    )(packed, *slots)


def finish_kernel(count, step, begin, packed, total, *refs):
    slots, out_at, out, sems = refs[:count], *refs[count:]
    rows, width = out.shape
    matrix = mixing(packed, width, begin, count * CAP)

    def copy(i):
        at = pl.ds(i * step, step)
        return pltpu.make_async_copy(out.at[:, at], out_at.at[:, at], sems.at[i])

    for i in range(width // step):
        at = pl.ds(i * step, step)
        stacked = jnp.concatenate([s[:, at].astype(F32) for s in slots], axis=0)
        out[:, at] = (total[:, at] + mixed(matrix, stacked)).astype(BF16)
        copy(i).start()
    for i in range(width // step):
        copy(i).wait()


def finish_combine(packed, total, slots, begin):
    count = len(slots)
    rows, width = total.shape
    step = chunk_of(width, 512)
    return pl.pallas_call(
        functools.partial(finish_kernel, count, step, begin),
        out_shape=jax.ShapeDtypeStruct((rows, width), BF16),
        in_specs=[VMEM] * (count + 2),
        out_specs=HBM,
        scratch_shapes=[
            pltpu.VMEM((rows, width), BF16),
            pltpu.SemaphoreType.DMA((width // step,)),
        ],
        compiler_params=pltpu.CompilerParams(vmem_limit_bytes=8 << 20),
    )(packed, total, *slots)


def shards(hidden, norm_gain, expert_ids, gate_weights, expert_gate_up, expert_down, partner):
    devices = lax.axis_size("ep")
    sections = lax.axis_size("pp")
    section_rows = hidden[0]
    gate_up = expert_gate_up[0, 0]
    down = expert_down[0, 0]

    far, split = devices // 2, max(1, devices * 3 // 4)
    early = [far] + [k for k in range(1, split) if k != far]
    late = list(range(split, devices))
    ids, gates = expert_ids[0].T, gate_weights[0].T
    *picked, rows = route_first(section_rows, ids, devices, early)
    *rest, packed, gain, gate_up = route_rest(
        rows,
        ids,
        gates,
        partner,
        norm_gain,
        gate_up,
        devices,
        late + [0],
        early[::-1] + late + [0],
    )
    picked = dict(zip(early + late + [0], picked + rest))

    def onward(value):
        return lax.ppermute(value, "pp", [(i, (i + 1) % sections) for i in range(sections)])

    def dispatch(value, offset):
        if offset == 0:
            return value
        return lax.ppermute(
            value, "ep", [(i, offset_target(i, offset, devices)) for i in range(devices)]
        )

    def send_back(value, offset):
        return lax.ppermute(
            value,
            ("ep", "pp"),
            [
                (offset_target(i, offset, devices) * sections + p, i * sections + (p + 1) % sections)
                for i in range(devices)
                for p in range(sections)
            ],
        )

    arrived = {k: dispatch(picked[k], k) for k in early + late + [0]}
    packed = onward(packed)
    results, down = early_experts([arrived[k] for k in early + [0]], gain, gate_up, down)
    results = dict(zip(early + [0], results))
    returned = {k: send_back(results[k], k) for k in early[::-1]}
    packed, *held = lax.optimization_barrier((packed, *[arrived[k] for k in late]))
    results.update(zip(late, late_experts(held, gain, gate_up, down)))
    last = late + [0]
    for k, result in zip(last, lax.optimization_barrier([results[k] for k in last])):
        returned[k] = send_back(result, k)
    total = begin_combine(packed, [returned[k] for k in early[::-1]])
    begin = section_rows.shape[0] + len(early) * CAP
    out = finish_combine(packed, total, [returned[k] for k in late + [0]], begin)
    return out[None]


def solution(mesh):
    return jax.shard_map(
        shards,
        mesh=mesh,
        in_specs=(
            P("pp", ("grp", "ep"), None),
            P("pp", None),
            P("pp", ("grp", "ep"), None),
            P("pp", ("grp", "ep"), None),
            P("pp", "ep", None, None),
            P("pp", "ep", None, None),
            P(("grp", "ep"), None),
        ),
        out_specs=P("pp", ("grp", "ep"), None),
        check_vma=False,
    )
```

time: 38.4 us -> 37.4 us (0.974)
  starting transfers between devices: 9.2 us -> 10.3 us
  Pallas kernels: 17.4 us -> 16.4 us
  waiting for transfers between devices: 11.5 us -> 10.5 us
    ppermute x1, starting transfers between devices: 0.08 us -> 2.37 us  [onward(): lax.ppermute(value, 'pp', [(i, (i + 1) % sections) for i in range(section...]
    ppermute x3 -> x4, starting transfers between devices: 6.32 us -> 5.23 us  [send_back(): lax.ppermute(value, ('ep', 'pp'), [(offset_target(i, offset, devices) * s...]
    pallas_call x1, Pallas kernels: 1.93 us -> 1.2 us  [route_first(): pl.pallas_call(functools.partial(first_kernel, devices, offsets), out_sha...]
    ppermute x3 -> x4, waiting for transfers between devices: 10.3 us -> 9.73 us  [send_back(): lax.ppermute(value, ('ep', 'pp'), [(offset_target(i, offset, devices) * s...]
    ppermute x3, waiting for transfers between devices: 1.23 us -> 0.8 us  [dispatch(): lax.ppermute(value, 'ep', [(i, offset_target(i, offset, devices)) for i i...]
    pallas_call x2 -> x3, Pallas kernels: 7.06 us -> 6.68 us  [the longest x1 5.4 us: route_rest(): pl.pallas_call(functools.partial(rest_kernel, devices, offsets, order, pa...]
  transfers between devices with their start and end apart: 7 -> 8, of which waited for: 3 -> 3; matrix products, arithmetic and copies ran while one was open for 0% -> 0% of each run, Pallas kernels for 38% -> 38%
where the time goes in v4:
time: 37.4 us; the launch traced here: 37.2 us
  Pallas kernels  16.4 us (44%)
  waiting for transfers between devices  10.5 us (28%)
  starting transfers between devices  10.3 us (28%)
    ppermute x4, waiting for transfers between devices, send_back(): lax.ppermute(value, ('ep', 'pp'), [(offset_target(i, offset, devices) * s...  9.73 us
    pallas_call x1, Pallas kernels, route_rest(): pl.pallas_call(functools.partial(rest_kernel, devices, offsets, order, pa...  5.4 us
    ppermute x4, starting transfers between devices, send_back(): lax.ppermute(value, ('ep', 'pp'), [(offset_target(i, offset, devices) * s...  5.23 us
    pallas_call x1, Pallas kernels, early_experts(): pl.pallas_call(functools.partial(early_kernel, count, chunk_of(width, 512...  4.48 us
    pallas_call x1, Pallas kernels, late_experts(): pl.pallas_call(functools.partial(late_kernel, count, chunk_of(width, 512)...  4.01 us
    ppermute x3, starting transfers between devices, dispatch(): lax.ppermute(value, 'ep', [(i, offset_target(i, offset, devices)) for i i...  2.72 us
    ppermute x1, starting transfers between devices, onward(): lax.ppermute(value, 'pp', [(i, (i + 1) % sections) for i in range(section...  2.37 us
    pallas_call x1, Pallas kernels, route_first(): pl.pallas_call(functools.partial(first_kernel, devices, offsets), out_sha...  1.2 us
  transfers between devices with their start and end apart: 8, of which 3 were waited for; matrix products, arithmetic and copies ran while one was open for 0% of the time, Pallas kernels for 38%

profile of v4, /device:TPU:9, one launch (start us, length us, event | category | flops | bytes accessed | tf_op | source)
XLA Modules:
  0.0 37.2 jit_solution(2919975422210009200)
XLA Ops:
  0.0 1.2 %shard_map.73 = (bf16[24,3584]{1,0:T(8,128)(2,1)S(1)}, bf16[24,3584]{1,0:T(8,128)(2,1)S(1)}, bf16[32,3584]{1,0:T(8,128)(2,1)S(1)}) custom-call(bf16[32,3584]{1,0:T(8,128)(2,1)} %bitcast.12, s32[2,32]{1,0:T(2,128)} %bitcast.13), custom_call_target="tpu_custom_call" | custom-call | tf_op jit(solution)/shard_map/pallas_call | solution.py:99
  1.2 2.4 %collective-permute-start.2 = (bf16[24,3584]{1,0:T(8,128)(2,1)S(1)}, bf16[24,3584]{1,0:T(8,128)(2,1)S(1)}, u32[]{:S(2)}, u32[]{:S(2)}) collective-permute-start(bf16[24,3584]{1,0:T(8,128)(2,1)S(1)} %get-tuple-element.25), channel_id=1, source_target_pairs={{0,8},{4,12},{8,0},{12,4},{1,9},{5,13},{9,1},{13,5},{2,10},{6,14},... | collective-permute-start | bytes 516104 | tf_op jit(solution)/shard_map/ppermute | solution.py:380
  3.6 0.2 collective-permute-start.3
  3.8 5.4 %shard_map.74 = (bf16[24,3584]{1,0:T(8,128)(2,1)S(1)}, bf16[24,3584]{1,0:T(8,128)(2,1)S(1)}, bf16[32,3840]{1,0:T(8,128)(2,1)S(1)}, bf16[1,3584]{1,0:T(2,128)(2,1)S(1)}, bf16[3584,2048]{1,0:T(8,128)(2,1)S(1)}) custom-call(bf16[32,3584]{1,0:T(8,128)(2,1)S(1)} %get-tuple-element.21.hidden, s32[2,32]{1,0:T(2,128)} %bitcast.14, f32[2,32]{1,0:T(2,128)} %bitcast.15, ...), custom_call_target="tpu_custom_call" | custom-call | bytes 14680064 | tf_op jit(solution)/shard_map/pallas_call | solution.py:183
  9.2 2.4 %collective-permute-start = (bf16[32,3840]{1,0:T(8,128)(2,1)S(1)}, bf16[32,3840]{1,0:T(8,128)(2,1)S(1)}, u32[]{:S(2)}, u32[]{:S(2)}) collective-permute-start(bf16[32,3840]{1,0:T(8,128)(2,1)S(1)} %get-tuple-element.22), channel_id=1, source_target_pairs={{0,1},{1,2},{2,3},{3,0},{4,5},{5,6},{6,7},{7,4},{8,9},{9,10},{10,1... | collective-permute-start | bytes 737288 | tf_op jit(solution)/shard_map/ppermute | solution.py:375
  11.5 0.2 collective-permute-start.1
  11.7 0.0 collective-permute-done.2.refs_0_
  11.7 0.0 collective-permute-done.3.refs_1_
  11.7 4.5 %shard_map.75 = (bf16[24,3584]{1,0:T(8,128)(2,1)S(1)}, bf16[24,3584]{1,0:T(8,128)(2,1)S(1)}, bf16[24,3584]{1,0:T(8,128)(2,1)S(1)}, bf16[1024,3584]{1,0:T(8,128)(2,1)S(1)}) custom-call(bf16[24,3584]{1,0:T(8,128)(2,1)S(1)} %collective-permute-done.2.refs_0_, bf16[24,3584]{1,0:T(8,128)(2,1)S(1)} %collective-permute-done.3.refs_1_, ...), custom_call_target="tpu_custom_call" | custom-call | flops 1585446912 | bytes 22020096 | tf_op jit(solution)/shard_map/pallas_call | solution.py:232
  16.2 2.3 %collective-permute-start.4 = (bf16[24,3584]{1,0:T(8,128)(2,1)S(1)}, bf16[24,3584]{1,0:T(8,128)(2,1)S(1)}, u32[]{:S(2)}, u32[]{:S(2)}) collective-permute-start(bf16[24,3584]{1,0:T(8,128)(2,1)S(1)} %get-tuple-element.30), channel_id=1, source_target_pairs={{4,1},{5,2},{6,3},{7,0},{0,5},{1,6},{2,7},{3,4},{12,9},{13,10},{14... | collective-permute-start | bytes 516104 | tf_op jit(solution)/shard_map/ppermute | solution.py:385
  18.5 1.8 %collective-permute-start.5 = (bf16[24,3584]{1,0:T(8,128)(2,1)S(1)}, bf16[24,3584]{1,0:T(8,128)(2,1)S(1)}, u32[]{:S(2)}, u32[]{:S(2)}) collective-permute-start(bf16[24,3584]{1,0:T(8,128)(2,1)S(1)} %get-tuple-element.31), channel_id=1, source_target_pairs={{8,1},{9,2},{10,3},{11,0},{12,5},{13,6},{14,7},{15,4},{0,9},{1,10}... | collective-permute-start | bytes 516104 | tf_op jit(solution)/shard_map/ppermute | solution.py:385
  20.3 0.8 %collective-permute-done.1.refs_0_ = bf16[24,3584]{1,0:T(8,128)(2,1)S(1)} collective-permute-done((bf16[24,3584]{1,0:T(8,128)(2,1)S(1)}, bf16[24,3584]{1,0:T(8,128)(2,1)S(1)}, u32[]{:S(2)}, u32[]{:S(2)}) %collective-permute-start.1) | collective-permute-done | bytes 172064 | tf_op jit(solution)/shard_map/ppermute | solution.py:380
  21.1 0.0 collective-permute-done.packed
  21.1 4.0 %shard_map.77 = bf16[24,3584]{1,0:T(8,128)(2,1)S(1)} custom-call(bf16[24,3584]{1,0:T(8,128)(2,1)S(1)} %collective-permute-done.1.refs_0_, bf16[1,3584]{1,0:T(2,128)(2,1)S(1)} %get-tuple-element.28.refs_3_.refs_1_, bf16[3584,2048]{1,0:T(8,128)(2,1)S(1)} %get-tuple-element.29.refs_4_.refs_2_, bf16[1024,3584]{1,0:T(8,128)(2,1)S(1)} %get-tuple-element.33.refs_3_), custom_call_target="tpu_custom_call" | custom-call | flops 4227858432 | bytes 176160768 | tf_op jit(solution)/shard_map/pallas_call | solution.py:263
  25.1 1.1 %collective-permute-start.6 = (bf16[24,3584]{1,0:T(8,128)(2,1)S(1)}, bf16[24,3584]{1,0:T(8,128)(2,1)S(1)}, u32[]{:S(2)}, u32[]{:S(2)}) collective-permute-start(bf16[24,3584]{1,0:T(8,128)(2,1)S(1)} %shard_map.77), channel_id=1, source_target_pairs={{12,1},{13,2},{14,3},{15,0},{8,5},{9,6},{10,7},{11,4},{4,9},{5,10}... | collective-permute-start | bytes 516104 | tf_op jit(solution)/shard_map/ppermute | solution.py:385
  26.2 0.1 collective-permute-start.7
  26.2 0.0 collective-permute-done.4.refs_0_
  26.2 5.6 %collective-permute-done.5.refs_1_ = bf16[24,3584]{1,0:T(8,128)(2,1)S(1)} collective-permute-done((bf16[24,3584]{1,0:T(8,128)(2,1)S(1)}, bf16[24,3584]{1,0:T(8,128)(2,1)S(1)}, u32[]{:S(2)}, u32[]{:S(2)}) %collective-permute-start.5) | collective-permute-done | bytes 172064 | tf_op jit(solution)/shard_map/ppermute | solution.py:385
  31.9 0.3 shard_map.76.total
  32.2 4.1 %collective-permute-done.6.refs_0_ = bf16[24,3584]{1,0:T(8,128)(2,1)S(1)} collective-permute-done((bf16[24,3584]{1,0:T(8,128)(2,1)S(1)}, bf16[24,3584]{1,0:T(8,128)(2,1)S(1)}, u32[]{:S(2)}, u32[]{:S(2)}) %collective-permute-start.6) | collective-permute-done | bytes 172064 | tf_op jit(solution)/shard_map/ppermute | solution.py:385
  36.2 0.0 collective-permute-done.7.refs_1_
  36.2 1.0 %shard_map.78 = bf16[32,3584]{1,0:T(8,128)(2,1)} custom-call(bf16[32,3840]{1,0:T(8,128)(2,1)S(1)} %collective-permute-done.packed, f32[32,3584]{1,0:T(8,128)S(1)} %shard_map.76.total, bf16[24,3584]{1,0:T(8,128)(2,1)S(1)} %collective-permute-done.6.refs_0_, bf16[24,3584]{1,0:T(8,128)(2,1)S(1)} %collective-permute-done.7.refs_1_), custom_call_target="tpu_custom_call" | custom-call | tf_op jit(solution)/shard_map/pallas_call | solution.py:336
Async XLA Ops:
  1.2 10.5 %collective-permute-start.2 = (bf16[24,3584]{1,0:T(8,128)(2,1)S(1)}, bf16[24,3584]{1,0:T(8,128)(2,1)S(1)}, u32[]{:S(2)}, u32[]{:S(2)}) collective-permute-start(bf16[24,3584]{1,0:T(8,128)(2,1)S(1)} %get-tuple-element.25), channel_id=1, source_target_pairs={{0,8},{4,12},{8,0},{12,4},{1,9},{5,13},{9,1},{13,5},{2,10},{6,14},... | collective-permute-start | bytes 516104 | tf_op jit(solution)/shard_map/ppermute | solution.py:380
  3.6 8.1 %collective-permute-start.3 = (bf16[24,3584]{1,0:T(8,128)(2,1)S(1)}, bf16[24,3584]{1,0:T(8,128)(2,1)S(1)}, u32[]{:S(2)}, u32[]{:S(2)}) collective-permute-start(bf16[24,3584]{1,0:T(8,128)(2,1)S(1)} %get-tuple-element.26), channel_id=1, source_target_pairs={{0,4},{4,0},{8,12},{12,8},{1,5},{5,1},{9,13},{13,9},{2,6},{6,2},{1... | collective-permute-start | bytes 516104 | tf_op jit(solution)/shard_map/ppermute | solution.py:380
  9.2 11.9 %collective-permute-start = (bf16[32,3840]{1,0:T(8,128)(2,1)S(1)}, bf16[32,3840]{1,0:T(8,128)(2,1)S(1)}, u32[]{:S(2)}, u32[]{:S(2)}) collective-permute-start(bf16[32,3840]{1,0:T(8,128)(2,1)S(1)} %get-tuple-element.22), channel_id=1, source_target_pairs={{0,1},{1,2},{2,3},{3,0},{4,5},{5,6},{6,7},{7,4},{8,9},{9,10},{10,1... | collective-permute-start | bytes 737288 | tf_op jit(solution)/shard_map/ppermute | solution.py:375
  11.5 9.5 %collective-permute-start.1 = (bf16[24,3584]{1,0:T(8,128)(2,1)S(1)}, bf16[24,3584]{1,0:T(8,128)(2,1)S(1)}, u32[]{:S(2)}, u32[]{:S(2)}) collective-permute-start(bf16[24,3584]{1,0:T(8,128)(2,1)S(1)} %get-tuple-element.23), channel_id=1, source_target_pairs={{0,12},{4,8},{8,4},{12,0},{1,13},{5,9},{9,5},{13,1},{2,14},{6,10},... | collective-permute-start | bytes 516104 | tf_op jit(solution)/shard_map/ppermute | solution.py:380
  16.2 10.0 %collective-permute-start.4 = (bf16[24,3584]{1,0:T(8,128)(2,1)S(1)}, bf16[24,3584]{1,0:T(8,128)(2,1)S(1)}, u32[]{:S(2)}, u32[]{:S(2)}) collective-permute-start(bf16[24,3584]{1,0:T(8,128)(2,1)S(1)} %get-tuple-element.30), channel_id=1, source_target_pairs={{4,1},{5,2},{6,3},{7,0},{0,5},{1,6},{2,7},{3,4},{12,9},{13,10},{14... | collective-permute-start | bytes 516104 | tf_op jit(solution)/shard_map/ppermute | solution.py:385
  18.5 13.4 %collective-permute-start.5 = (bf16[24,3584]{1,0:T(8,128)(2,1)S(1)}, bf16[24,3584]{1,0:T(8,128)(2,1)S(1)}, u32[]{:S(2)}, u32[]{:S(2)}) collective-permute-start(bf16[24,3584]{1,0:T(8,128)(2,1)S(1)} %get-tuple-element.31), channel_id=1, source_target_pairs={{8,1},{9,2},{10,3},{11,0},{12,5},{13,6},{14,7},{15,4},{0,9},{1,10}... | collective-permute-start | bytes 516104 | tf_op jit(solution)/shard_map/ppermute | solution.py:385
  25.1 11.2 %collective-permute-start.6 = (bf16[24,3584]{1,0:T(8,128)(2,1)S(1)}, bf16[24,3584]{1,0:T(8,128)(2,1)S(1)}, u32[]{:S(2)}, u32[]{:S(2)}) collective-permute-start(bf16[24,3584]{1,0:T(8,128)(2,1)S(1)} %shard_map.77), channel_id=1, source_target_pairs={{12,1},{13,2},{14,3},{15,0},{8,5},{9,6},{10,7},{11,4},{4,9},{5,10}... | collective-permute-start | bytes 516104 | tf_op jit(solution)/shard_map/ppermute | solution.py:385
  26.2 10.1 %collective-permute-start.7 = (bf16[24,3584]{1,0:T(8,128)(2,1)S(1)}, bf16[24,3584]{1,0:T(8,128)(2,1)S(1)}, u32[]{:S(2)}, u32[]{:S(2)}) collective-permute-start(bf16[24,3584]{1,0:T(8,128)(2,1)S(1)} %get-tuple-element.36), channel_id=1, source_target_pairs={{0,1},{1,2},{2,3},{3,0},{4,5},{5,6},{6,7},{7,4},{8,9},{9,10},{10,1... | collective-permute-start | bytes 516104 | tf_op jit(solution)/shard_map/ppermute | solution.py:385

commit v5 on v4

--- a/solution.py
+++ b/solution.py
@@ -332,7 +332,7 @@
 def finish_combine(packed, total, slots, begin):
     count = len(slots)
     rows, width = total.shape
-    step = chunk_of(width, 512)
+    step = chunk_of(width, 1792)
     return pl.pallas_call(
         functools.partial(finish_kernel, count, step, begin),
         out_shape=jax.ShapeDtypeStruct((rows, width), BF16),

time: 37.4 us -> 37.4 us (level)
  no operation moved by 1% of the time
where the time goes in v5:
time: 37.4 us; the launch traced here: 37.2 us
  Pallas kernels  16.3 us (44%)
  waiting for transfers between devices  10.5 us (28%)
  starting transfers between devices  10.3 us (28%)
    ppermute x4, waiting for transfers between devices, send_back(): lax.ppermute(value, ('ep', 'pp'), [(offset_target(i, offset, devices) * s...  9.73 us
    pallas_call x1, Pallas kernels, route_rest(): pl.pallas_call(functools.partial(rest_kernel, devices, offsets, order, pa...  5.4 us
    ppermute x4, starting transfers between devices, send_back(): lax.ppermute(value, ('ep', 'pp'), [(offset_target(i, offset, devices) * s...  5.23 us
    pallas_call x1, Pallas kernels, early_experts(): pl.pallas_call(functools.partial(early_kernel, count, chunk_of(width, 512...  4.48 us
    pallas_call x1, Pallas kernels, late_experts(): pl.pallas_call(functools.partial(late_kernel, count, chunk_of(width, 512)...  4.01 us
    ppermute x3, starting transfers between devices, dispatch(): lax.ppermute(value, 'ep', [(i, offset_target(i, offset, devices)) for i i...  2.72 us
    ppermute x1, starting transfers between devices, onward(): lax.ppermute(value, 'pp', [(i, (i + 1) % sections) for i in range(section...  2.37 us
    pallas_call x1, Pallas kernels, route_first(): pl.pallas_call(functools.partial(first_kernel, devices, offsets), out_sha...  1.2 us
  transfers between devices with their start and end apart: 8, of which 3 were waited for; matrix products, arithmetic and copies ran while one was open for 0% of the time, Pallas kernels for 38%

profile of v5, /device:TPU:9, one launch (start us, length us, event | category | flops | bytes accessed | tf_op | source)
XLA Modules:
  0.0 37.2 jit_solution(3220712374844819386)
XLA Ops:
  0.0 1.2 %shard_map.73 = (bf16[24,3584]{1,0:T(8,128)(2,1)S(1)}, bf16[24,3584]{1,0:T(8,128)(2,1)S(1)}, bf16[32,3584]{1,0:T(8,128)(2,1)S(1)}) custom-call(bf16[32,3584]{1,0:T(8,128)(2,1)} %bitcast.12, s32[2,32]{1,0:T(2,128)} %bitcast.13), custom_call_target="tpu_custom_call" | custom-call | tf_op jit(solution)/shard_map/pallas_call | solution.py:99
  1.2 2.4 %collective-permute-start.2 = (bf16[24,3584]{1,0:T(8,128)(2,1)S(1)}, bf16[24,3584]{1,0:T(8,128)(2,1)S(1)}, u32[]{:S(2)}, u32[]{:S(2)}) collective-permute-start(bf16[24,3584]{1,0:T(8,128)(2,1)S(1)} %get-tuple-element.25), channel_id=1, source_target_pairs={{0,8},{4,12},{8,0},{12,4},{1,9},{5,13},{9,1},{13,5},{2,10},{6,14},... | collective-permute-start | bytes 516104 | tf_op jit(solution)/shard_map/ppermute | solution.py:380
  3.6 0.2 collective-permute-start.3
  3.8 5.4 %shard_map.74 = (bf16[24,3584]{1,0:T(8,128)(2,1)S(1)}, bf16[24,3584]{1,0:T(8,128)(2,1)S(1)}, bf16[32,3840]{1,0:T(8,128)(2,1)S(1)}, bf16[1,3584]{1,0:T(2,128)(2,1)S(1)}, bf16[3584,2048]{1,0:T(8,128)(2,1)S(1)}) custom-call(bf16[32,3584]{1,0:T(8,128)(2,1)S(1)} %get-tuple-element.21.hidden, s32[2,32]{1,0:T(2,128)} %bitcast.14, f32[2,32]{1,0:T(2,128)} %bitcast.15, ...), custom_call_target="tpu_custom_call" | custom-call | bytes 14680064 | tf_op jit(solution)/shard_map/pallas_call | solution.py:183
  9.2 2.4 %collective-permute-start = (bf16[32,3840]{1,0:T(8,128)(2,1)S(1)}, bf16[32,3840]{1,0:T(8,128)(2,1)S(1)}, u32[]{:S(2)}, u32[]{:S(2)}) collective-permute-start(bf16[32,3840]{1,0:T(8,128)(2,1)S(1)} %get-tuple-element.22), channel_id=1, source_target_pairs={{0,1},{1,2},{2,3},{3,0},{4,5},{5,6},{6,7},{7,4},{8,9},{9,10},{10,1... | collective-permute-start | bytes 737288 | tf_op jit(solution)/shard_map/ppermute | solution.py:375
  11.5 0.2 collective-permute-start.1
  11.7 0.0 collective-permute-done.2.refs_0_
  11.7 0.0 collective-permute-done.3.refs_1_
  11.7 4.5 %shard_map.75 = (bf16[24,3584]{1,0:T(8,128)(2,1)S(1)}, bf16[24,3584]{1,0:T(8,128)(2,1)S(1)}, bf16[24,3584]{1,0:T(8,128)(2,1)S(1)}, bf16[1024,3584]{1,0:T(8,128)(2,1)S(1)}) custom-call(bf16[24,3584]{1,0:T(8,128)(2,1)S(1)} %collective-permute-done.2.refs_0_, bf16[24,3584]{1,0:T(8,128)(2,1)S(1)} %collective-permute-done.3.refs_1_, ...), custom_call_target="tpu_custom_call" | custom-call | flops 1585446912 | bytes 22020096 | tf_op jit(solution)/shard_map/pallas_call | solution.py:232
  16.2 2.3 %collective-permute-start.4 = (bf16[24,3584]{1,0:T(8,128)(2,1)S(1)}, bf16[24,3584]{1,0:T(8,128)(2,1)S(1)}, u32[]{:S(2)}, u32[]{:S(2)}) collective-permute-start(bf16[24,3584]{1,0:T(8,128)(2,1)S(1)} %get-tuple-element.30), channel_id=1, source_target_pairs={{4,1},{5,2},{6,3},{7,0},{0,5},{1,6},{2,7},{3,4},{12,9},{13,10},{14... | collective-permute-start | bytes 516104 | tf_op jit(solution)/shard_map/ppermute | solution.py:385
  18.5 1.8 %collective-permute-start.5 = (bf16[24,3584]{1,0:T(8,128)(2,1)S(1)}, bf16[24,3584]{1,0:T(8,128)(2,1)S(1)}, u32[]{:S(2)}, u32[]{:S(2)}) collective-permute-start(bf16[24,3584]{1,0:T(8,128)(2,1)S(1)} %get-tuple-element.31), channel_id=1, source_target_pairs={{8,1},{9,2},{10,3},{11,0},{12,5},{13,6},{14,7},{15,4},{0,9},{1,10}... | collective-permute-start | bytes 516104 | tf_op jit(solution)/shard_map/ppermute | solution.py:385
  20.3 0.8 %collective-permute-done.1.refs_0_ = bf16[24,3584]{1,0:T(8,128)(2,1)S(1)} collective-permute-done((bf16[24,3584]{1,0:T(8,128)(2,1)S(1)}, bf16[24,3584]{1,0:T(8,128)(2,1)S(1)}, u32[]{:S(2)}, u32[]{:S(2)}) %collective-permute-start.1) | collective-permute-done | bytes 172064 | tf_op jit(solution)/shard_map/ppermute | solution.py:380
  21.1 0.0 collective-permute-done.packed
  21.1 4.0 %shard_map.77 = bf16[24,3584]{1,0:T(8,128)(2,1)S(1)} custom-call(bf16[24,3584]{1,0:T(8,128)(2,1)S(1)} %collective-permute-done.1.refs_0_, bf16[1,3584]{1,0:T(2,128)(2,1)S(1)} %get-tuple-element.28.refs_3_.refs_1_, bf16[3584,2048]{1,0:T(8,128)(2,1)S(1)} %get-tuple-element.29.refs_4_.refs_2_, bf16[1024,3584]{1,0:T(8,128)(2,1)S(1)} %get-tuple-element.33.refs_3_), custom_call_target="tpu_custom_call" | custom-call | flops 4227858432 | bytes 176160768 | tf_op jit(solution)/shard_map/pallas_call | solution.py:263
  25.1 1.1 %collective-permute-start.6 = (bf16[24,3584]{1,0:T(8,128)(2,1)S(1)}, bf16[24,3584]{1,0:T(8,128)(2,1)S(1)}, u32[]{:S(2)}, u32[]{:S(2)}) collective-permute-start(bf16[24,3584]{1,0:T(8,128)(2,1)S(1)} %shard_map.77), channel_id=1, source_target_pairs={{12,1},{13,2},{14,3},{15,0},{8,5},{9,6},{10,7},{11,4},{4,9},{5,10}... | collective-permute-start | bytes 516104 | tf_op jit(solution)/shard_map/ppermute | solution.py:385
  26.2 0.1 collective-permute-start.7
  26.2 0.0 collective-permute-done.4.refs_0_
  26.2 5.6 %collective-permute-done.5.refs_1_ = bf16[24,3584]{1,0:T(8,128)(2,1)S(1)} collective-permute-done((bf16[24,3584]{1,0:T(8,128)(2,1)S(1)}, bf16[24,3584]{1,0:T(8,128)(2,1)S(1)}, u32[]{:S(2)}, u32[]{:S(2)}) %collective-permute-start.5) | collective-permute-done | bytes 172064 | tf_op jit(solution)/shard_map/ppermute | solution.py:385
  31.9 0.3 shard_map.76.total
  32.2 4.1 %collective-permute-done.6.refs_0_ = bf16[24,3584]{1,0:T(8,128)(2,1)S(1)} collective-permute-done((bf16[24,3584]{1,0:T(8,128)(2,1)S(1)}, bf16[24,3584]{1,0:T(8,128)(2,1)S(1)}, u32[]{:S(2)}, u32[]{:S(2)}) %collective-permute-start.6) | collective-permute-done | bytes 172064 | tf_op jit(solution)/shard_map/ppermute | solution.py:385
  36.2 0.0 collective-permute-done.7.refs_1_
  36.2 1.0 %shard_map.78 = bf16[32,3584]{1,0:T(8,128)(2,1)} custom-call(bf16[32,3840]{1,0:T(8,128)(2,1)S(1)} %collective-permute-done.packed, f32[32,3584]{1,0:T(8,128)S(1)} %shard_map.76.total, bf16[24,3584]{1,0:T(8,128)(2,1)S(1)} %collective-permute-done.6.refs_0_, bf16[24,3584]{1,0:T(8,128)(2,1)S(1)} %collective-permute-done.7.refs_1_), custom_call_target="tpu_custom_call" | custom-call | tf_op jit(solution)/shard_map/pallas_call | solution.py:336
Async XLA Ops:
  1.2 10.5 %collective-permute-start.2 = (bf16[24,3584]{1,0:T(8,128)(2,1)S(1)}, bf16[24,3584]{1,0:T(8,128)(2,1)S(1)}, u32[]{:S(2)}, u32[]{:S(2)}) collective-permute-start(bf16[24,3584]{1,0:T(8,128)(2,1)S(1)} %get-tuple-element.25), channel_id=1, source_target_pairs={{0,8},{4,12},{8,0},{12,4},{1,9},{5,13},{9,1},{13,5},{2,10},{6,14},... | collective-permute-start | bytes 516104 | tf_op jit(solution)/shard_map/ppermute | solution.py:380
  3.6 8.1 %collective-permute-start.3 = (bf16[24,3584]{1,0:T(8,128)(2,1)S(1)}, bf16[24,3584]{1,0:T(8,128)(2,1)S(1)}, u32[]{:S(2)}, u32[]{:S(2)}) collective-permute-start(bf16[24,3584]{1,0:T(8,128)(2,1)S(1)} %get-tuple-element.26), channel_id=1, source_target_pairs={{0,4},{4,0},{8,12},{12,8},{1,5},{5,1},{9,13},{13,9},{2,6},{6,2},{1... | collective-permute-start | bytes 516104 | tf_op jit(solution)/shard_map/ppermute | solution.py:380
  9.2 11.9 %collective-permute-start = (bf16[32,3840]{1,0:T(8,128)(2,1)S(1)}, bf16[32,3840]{1,0:T(8,128)(2,1)S(1)}, u32[]{:S(2)}, u32[]{:S(2)}) collective-permute-start(bf16[32,3840]{1,0:T(8,128)(2,1)S(1)} %get-tuple-element.22), channel_id=1, source_target_pairs={{0,1},{1,2},{2,3},{3,0},{4,5},{5,6},{6,7},{7,4},{8,9},{9,10},{10,1... | collective-permute-start | bytes 737288 | tf_op jit(solution)/shard_map/ppermute | solution.py:375
  11.5 9.5 %collective-permute-start.1 = (bf16[24,3584]{1,0:T(8,128)(2,1)S(1)}, bf16[24,3584]{1,0:T(8,128)(2,1)S(1)}, u32[]{:S(2)}, u32[]{:S(2)}) collective-permute-start(bf16[24,3584]{1,0:T(8,128)(2,1)S(1)} %get-tuple-element.23), channel_id=1, source_target_pairs={{0,12},{4,8},{8,4},{12,0},{1,13},{5,9},{9,5},{13,1},{2,14},{6,10},... | collective-permute-start | bytes 516104 | tf_op jit(solution)/shard_map/ppermute | solution.py:380
  16.2 10.0 %collective-permute-start.4 = (bf16[24,3584]{1,0:T(8,128)(2,1)S(1)}, bf16[24,3584]{1,0:T(8,128)(2,1)S(1)}, u32[]{:S(2)}, u32[]{:S(2)}) collective-permute-start(bf16[24,3584]{1,0:T(8,128)(2,1)S(1)} %get-tuple-element.30), channel_id=1, source_target_pairs={{4,1},{5,2},{6,3},{7,0},{0,5},{1,6},{2,7},{3,4},{12,9},{13,10},{14... | collective-permute-start | bytes 516104 | tf_op jit(solution)/shard_map/ppermute | solution.py:385
  18.5 13.4 %collective-permute-start.5 = (bf16[24,3584]{1,0:T(8,128)(2,1)S(1)}, bf16[24,3584]{1,0:T(8,128)(2,1)S(1)}, u32[]{:S(2)}, u32[]{:S(2)}) collective-permute-start(bf16[24,3584]{1,0:T(8,128)(2,1)S(1)} %get-tuple-element.31), channel_id=1, source_target_pairs={{8,1},{9,2},{10,3},{11,0},{12,5},{13,6},{14,7},{15,4},{0,9},{1,10}... | collective-permute-start | bytes 516104 | tf_op jit(solution)/shard_map/ppermute | solution.py:385
  25.1 11.2 %collective-permute-start.6 = (bf16[24,3584]{1,0:T(8,128)(2,1)S(1)}, bf16[24,3584]{1,0:T(8,128)(2,1)S(1)}, u32[]{:S(2)}, u32[]{:S(2)}) collective-permute-start(bf16[24,3584]{1,0:T(8,128)(2,1)S(1)} %shard_map.77), channel_id=1, source_target_pairs={{12,1},{13,2},{14,3},{15,0},{8,5},{9,6},{10,7},{11,4},{4,9},{5,10}... | collective-permute-start | bytes 516104 | tf_op jit(solution)/shard_map/ppermute | solution.py:385
  26.2 10.1 %collective-permute-start.7 = (bf16[24,3584]{1,0:T(8,128)(2,1)S(1)}, bf16[24,3584]{1,0:T(8,128)(2,1)S(1)}, u32[]{:S(2)}, u32[]{:S(2)}) collective-permute-start(bf16[24,3584]{1,0:T(8,128)(2,1)S(1)} %get-tuple-element.36), channel_id=1, source_target_pairs={{0,1},{1,2},{2,3},{3,0},{4,5},{5,6},{6,7},{7,4},{8,9},{9,10},{10,1... | collective-permute-start | bytes 516104 | tf_op jit(solution)/shard_map/ppermute | solution.py:385

commit v6 on v4

--- a/solution.py
+++ b/solution.py
@@ -394,11 +394,11 @@
 
     arrived = {k: dispatch(picked[k], k) for k in early + late + [0]}
     packed = onward(packed)
-    results, down = early_experts([arrived[k] for k in early + [0]], gain, gate_up, down)
-    results = dict(zip(early + [0], results))
+    results, down = early_experts([arrived[k] for k in early], gain, gate_up, down)
+    results = dict(zip(early, results))
     returned = {k: send_back(results[k], k) for k in early[::-1]}
-    packed, *held = lax.optimization_barrier((packed, *[arrived[k] for k in late]))
-    results.update(zip(late, late_experts(held, gain, gate_up, down)))
+    packed, *held = lax.optimization_barrier((packed, *[arrived[k] for k in late + [0]]))
+    results.update(zip(late + [0], late_experts(held, gain, gate_up, down)))
     last = late + [0]
     for k, result in zip(last, lax.optimization_barrier([results[k] for k in last])):
         returned[k] = send_back(result, k)

time: 37.4 us -> 37.4 us (level)
  no operation moved by 1% of the time
where the time goes in v6:
time: 37.4 us; the launch traced here: 37.2 us
  Pallas kernels  16.4 us (44%)
  starting transfers between devices  10.4 us (28%)
  waiting for transfers between devices  10.4 us (28%)
    ppermute x4, waiting for transfers between devices, send_back(): lax.ppermute(value, ('ep', 'pp'), [(offset_target(i, offset, devices) * s...  9.62 us
    pallas_call x1, Pallas kernels, route_rest(): pl.pallas_call(functools.partial(rest_kernel, devices, offsets, order, pa...  5.4 us
    ppermute x4, starting transfers between devices, send_back(): lax.ppermute(value, ('ep', 'pp'), [(offset_target(i, offset, devices) * s...  5.28 us
    pallas_call x1, Pallas kernels, early_experts(): pl.pallas_call(functools.partial(early_kernel, count, chunk_of(width, 512...  4.46 us
    pallas_call x1, Pallas kernels, late_experts(): pl.pallas_call(functools.partial(late_kernel, count, chunk_of(width, 512)...  4.05 us
    ppermute x3, starting transfers between devices, dispatch(): lax.ppermute(value, 'ep', [(i, offset_target(i, offset, devices)) for i i...  2.72 us
    ppermute x1, starting transfers between devices, onward(): lax.ppermute(value, 'pp', [(i, (i + 1) % sections) for i in range(section...  2.37 us
    pallas_call x1, Pallas kernels, route_first(): pl.pallas_call(functools.partial(first_kernel, devices, offsets), out_sha...  1.2 us
  transfers between devices with their start and end apart: 8, of which 3 were waited for; matrix products, arithmetic and copies ran while one was open for 0% of the time, Pallas kernels for 38%

profile of v6, /device:TPU:9, one launch (start us, length us, event | category | flops | bytes accessed | tf_op | source)
XLA Modules:
  0.0 37.2 jit_solution(6445561295670040492)
XLA Ops:
  0.0 1.2 %shard_map.73 = (bf16[24,3584]{1,0:T(8,128)(2,1)S(1)}, bf16[24,3584]{1,0:T(8,128)(2,1)S(1)}, bf16[32,3584]{1,0:T(8,128)(2,1)S(1)}) custom-call(bf16[32,3584]{1,0:T(8,128)(2,1)} %bitcast.12, s32[2,32]{1,0:T(2,128)} %bitcast.13), custom_call_target="tpu_custom_call" | custom-call | tf_op jit(solution)/shard_map/pallas_call | solution.py:99
  1.2 2.4 %collective-permute-start.2 = (bf16[24,3584]{1,0:T(8,128)(2,1)S(1)}, bf16[24,3584]{1,0:T(8,128)(2,1)S(1)}, u32[]{:S(2)}, u32[]{:S(2)}) collective-permute-start(bf16[24,3584]{1,0:T(8,128)(2,1)S(1)} %get-tuple-element.26), channel_id=1, source_target_pairs={{0,8},{4,12},{8,0},{12,4},{1,9},{5,13},{9,1},{13,5},{2,10},{6,14},... | collective-permute-start | bytes 516104 | tf_op jit(solution)/shard_map/ppermute | solution.py:380
  3.6 0.2 collective-permute-start.3
  3.8 5.4 %shard_map.74 = (bf16[24,3584]{1,0:T(8,128)(2,1)S(1)}, bf16[24,3584]{1,0:T(8,128)(2,1)S(1)}, bf16[32,3840]{1,0:T(8,128)(2,1)S(1)}, bf16[1,3584]{1,0:T(2,128)(2,1)S(1)}, bf16[3584,2048]{1,0:T(8,128)(2,1)S(1)}) custom-call(bf16[32,3584]{1,0:T(8,128)(2,1)S(1)} %get-tuple-element.21.hidden, s32[2,32]{1,0:T(2,128)} %bitcast.14, f32[2,32]{1,0:T(2,128)} %bitcast.15, ...), custom_call_target="tpu_custom_call" | custom-call | bytes 14680064 | tf_op jit(solution)/shard_map/pallas_call | solution.py:183
  9.2 2.4 %collective-permute-start = (bf16[32,3840]{1,0:T(8,128)(2,1)S(1)}, bf16[32,3840]{1,0:T(8,128)(2,1)S(1)}, u32[]{:S(2)}, u32[]{:S(2)}) collective-permute-start(bf16[32,3840]{1,0:T(8,128)(2,1)S(1)} %get-tuple-element.22), channel_id=1, source_target_pairs={{0,1},{1,2},{2,3},{3,0},{4,5},{5,6},{6,7},{7,4},{8,9},{9,10},{10,1... | collective-permute-start | bytes 737288 | tf_op jit(solution)/shard_map/ppermute | solution.py:375
  11.5 0.2 collective-permute-start.1
  11.7 0.0 collective-permute-done.2.refs_0_
  11.7 0.0 collective-permute-done.3.refs_1_
  11.7 4.5 %shard_map.75 = (bf16[24,3584]{1,0:T(8,128)(2,1)S(1)}, bf16[24,3584]{1,0:T(8,128)(2,1)S(1)}, bf16[1024,3584]{1,0:T(8,128)(2,1)S(1)}) custom-call(bf16[24,3584]{1,0:T(8,128)(2,1)S(1)} %collective-permute-done.2.refs_0_, bf16[24,3584]{1,0:T(8,128)(2,1)S(1)} %collective-permute-done.3.refs_1_, bf16[1,3584]{1,0:T(2,128)(2,1)S(1)} %get-tuple-element.28.refs_2_, ...), custom_call_target="tpu_custom_call" | custom-call | flops 1056964608 | bytes 22020096 | tf_op jit(solution)/shard_map/pallas_call | solution.py:232
  16.2 2.3 %collective-permute-start.4 = (bf16[24,3584]{1,0:T(8,128)(2,1)S(1)}, bf16[24,3584]{1,0:T(8,128)(2,1)S(1)}, u32[]{:S(2)}, u32[]{:S(2)}) collective-permute-start(bf16[24,3584]{1,0:T(8,128)(2,1)S(1)} %get-tuple-element.30), channel_id=1, source_target_pairs={{4,1},{5,2},{6,3},{7,0},{0,5},{1,6},{2,7},{3,4},{12,9},{13,10},{14... | collective-permute-start | bytes 516104 | tf_op jit(solution)/shard_map/ppermute | solution.py:385
  18.4 1.8 %collective-permute-start.5 = (bf16[24,3584]{1,0:T(8,128)(2,1)S(1)}, bf16[24,3584]{1,0:T(8,128)(2,1)S(1)}, u32[]{:S(2)}, u32[]{:S(2)}) collective-permute-start(bf16[24,3584]{1,0:T(8,128)(2,1)S(1)} %get-tuple-element.31), channel_id=1, source_target_pairs={{8,1},{9,2},{10,3},{11,0},{12,5},{13,6},{14,7},{15,4},{0,9},{1,10}... | collective-permute-start | bytes 516104 | tf_op jit(solution)/shard_map/ppermute | solution.py:385
  20.3 0.8 %collective-permute-done.1.refs_0_ = bf16[24,3584]{1,0:T(8,128)(2,1)S(1)} collective-permute-done((bf16[24,3584]{1,0:T(8,128)(2,1)S(1)}, bf16[24,3584]{1,0:T(8,128)(2,1)S(1)}, u32[]{:S(2)}, u32[]{:S(2)}) %collective-permute-start.1) | collective-permute-done | bytes 172064 | tf_op jit(solution)/shard_map/ppermute | solution.py:380
  21.1 0.0 collective-permute-done.packed
  21.1 4.0 %shard_map.77 = (bf16[24,3584]{1,0:T(8,128)(2,1)S(1)}, bf16[24,3584]{1,0:T(8,128)(2,1)S(1)}) custom-call(bf16[24,3584]{1,0:T(8,128)(2,1)S(1)} %collective-permute-done.1.refs_0_, bf16[24,3584]{1,0:T(8,128)(2,1)S(1)} %get-tuple-element.33.refs_1_, bf16[1,3584]{1,0:T(2,128)(2,1)S(1)} %get-tuple-element.28.refs_2_, ...), custom_call_target="tpu_custom_call" | custom-call | flops 8455716864 | bytes 176160768 | tf_op jit(solution)/shard_map/pallas_call | solution.py:263
  25.1 1.1 %collective-permute-start.6 = (bf16[24,3584]{1,0:T(8,128)(2,1)S(1)}, bf16[24,3584]{1,0:T(8,128)(2,1)S(1)}, u32[]{:S(2)}, u32[]{:S(2)}) collective-permute-start(bf16[24,3584]{1,0:T(8,128)(2,1)S(1)} %get-tuple-element.35), channel_id=1, source_target_pairs={{12,1},{13,2},{14,3},{15,0},{8,5},{9,6},{10,7},{11,4},{4,9},{5,10}... | collective-permute-start | bytes 516104 | tf_op jit(solution)/shard_map/ppermute | solution.py:385
  26.2 0.1 collective-permute-start.7
  26.3 0.0 collective-permute-done.4.refs_0_
  26.3 5.5 %collective-permute-done.5.refs_1_ = bf16[24,3584]{1,0:T(8,128)(2,1)S(1)} collective-permute-done((bf16[24,3584]{1,0:T(8,128)(2,1)S(1)}, bf16[24,3584]{1,0:T(8,128)(2,1)S(1)}, u32[]{:S(2)}, u32[]{:S(2)}) %collective-permute-start.5) | collective-permute-done | bytes 172064 | tf_op jit(solution)/shard_map/ppermute | solution.py:385
  31.9 0.3 shard_map.76.total
  32.1 4.1 %collective-permute-done.6.refs_0_ = bf16[24,3584]{1,0:T(8,128)(2,1)S(1)} collective-permute-done((bf16[24,3584]{1,0:T(8,128)(2,1)S(1)}, bf16[24,3584]{1,0:T(8,128)(2,1)S(1)}, u32[]{:S(2)}, u32[]{:S(2)}) %collective-permute-start.6) | collective-permute-done | bytes 172064 | tf_op jit(solution)/shard_map/ppermute | solution.py:385
  36.2 0.0 collective-permute-done.7.refs_1_
  36.2 1.0 %shard_map.78 = bf16[32,3584]{1,0:T(8,128)(2,1)} custom-call(bf16[32,3840]{1,0:T(8,128)(2,1)S(1)} %collective-permute-done.packed, f32[32,3584]{1,0:T(8,128)S(1)} %shard_map.76.total, bf16[24,3584]{1,0:T(8,128)(2,1)S(1)} %collective-permute-done.6.refs_0_, bf16[24,3584]{1,0:T(8,128)(2,1)S(1)} %collective-permute-done.7.refs_1_), custom_call_target="tpu_custom_call" | custom-call | tf_op jit(solution)/shard_map/pallas_call | solution.py:336
Async XLA Ops:
  1.2 10.5 %collective-permute-start.2 = (bf16[24,3584]{1,0:T(8,128)(2,1)S(1)}, bf16[24,3584]{1,0:T(8,128)(2,1)S(1)}, u32[]{:S(2)}, u32[]{:S(2)}) collective-permute-start(bf16[24,3584]{1,0:T(8,128)(2,1)S(1)} %get-tuple-element.26), channel_id=1, source_target_pairs={{0,8},{4,12},{8,0},{12,4},{1,9},{5,13},{9,1},{13,5},{2,10},{6,14},... | collective-permute-start | bytes 516104 | tf_op jit(solution)/shard_map/ppermute | solution.py:380
  3.6 8.1 %collective-permute-start.3 = (bf16[24,3584]{1,0:T(8,128)(2,1)S(1)}, bf16[24,3584]{1,0:T(8,128)(2,1)S(1)}, u32[]{:S(2)}, u32[]{:S(2)}) collective-permute-start(bf16[24,3584]{1,0:T(8,128)(2,1)S(1)} %get-tuple-element.27), channel_id=1, source_target_pairs={{0,4},{4,0},{8,12},{12,8},{1,5},{5,1},{9,13},{13,9},{2,6},{6,2},{1... | collective-permute-start | bytes 516104 | tf_op jit(solution)/shard_map/ppermute | solution.py:380
  9.2 11.9 %collective-permute-start = (bf16[32,3840]{1,0:T(8,128)(2,1)S(1)}, bf16[32,3840]{1,0:T(8,128)(2,1)S(1)}, u32[]{:S(2)}, u32[]{:S(2)}) collective-permute-start(bf16[32,3840]{1,0:T(8,128)(2,1)S(1)} %get-tuple-element.22), channel_id=1, source_target_pairs={{0,1},{1,2},{2,3},{3,0},{4,5},{5,6},{6,7},{7,4},{8,9},{9,10},{10,1... | collective-permute-start | bytes 737288 | tf_op jit(solution)/shard_map/ppermute | solution.py:375
  11.5 9.5 %collective-permute-start.1 = (bf16[24,3584]{1,0:T(8,128)(2,1)S(1)}, bf16[24,3584]{1,0:T(8,128)(2,1)S(1)}, u32[]{:S(2)}, u32[]{:S(2)}) collective-permute-start(bf16[24,3584]{1,0:T(8,128)(2,1)S(1)} %get-tuple-element.23), channel_id=1, source_target_pairs={{0,12},{4,8},{8,4},{12,0},{1,13},{5,9},{9,5},{13,1},{2,14},{6,10},... | collective-permute-start | bytes 516104 | tf_op jit(solution)/shard_map/ppermute | solution.py:380
  16.2 10.2 %collective-permute-start.4 = (bf16[24,3584]{1,0:T(8,128)(2,1)S(1)}, bf16[24,3584]{1,0:T(8,128)(2,1)S(1)}, u32[]{:S(2)}, u32[]{:S(2)}) collective-permute-start(bf16[24,3584]{1,0:T(8,128)(2,1)S(1)} %get-tuple-element.30), channel_id=1, source_target_pairs={{4,1},{5,2},{6,3},{7,0},{0,5},{1,6},{2,7},{3,4},{12,9},{13,10},{14... | collective-permute-start | bytes 516104 | tf_op jit(solution)/shard_map/ppermute | solution.py:385
  18.4 13.4 %collective-permute-start.5 = (bf16[24,3584]{1,0:T(8,128)(2,1)S(1)}, bf16[24,3584]{1,0:T(8,128)(2,1)S(1)}, u32[]{:S(2)}, u32[]{:S(2)}) collective-permute-start(bf16[24,3584]{1,0:T(8,128)(2,1)S(1)} %get-tuple-element.31), channel_id=1, source_target_pairs={{8,1},{9,2},{10,3},{11,0},{12,5},{13,6},{14,7},{15,4},{0,9},{1,10}... | collective-permute-start | bytes 516104 | tf_op jit(solution)/shard_map/ppermute | solution.py:385
  25.1 11.1 %collective-permute-start.6 = (bf16[24,3584]{1,0:T(8,128)(2,1)S(1)}, bf16[24,3584]{1,0:T(8,128)(2,1)S(1)}, u32[]{:S(2)}, u32[]{:S(2)}) collective-permute-start(bf16[24,3584]{1,0:T(8,128)(2,1)S(1)} %get-tuple-element.35), channel_id=1, source_target_pairs={{12,1},{13,2},{14,3},{15,0},{8,5},{9,6},{10,7},{11,4},{4,9},{5,10}... | collective-permute-start | bytes 516104 | tf_op jit(solution)/shard_map/ppermute | solution.py:385
  26.2 10.0 %collective-permute-start.7 = (bf16[24,3584]{1,0:T(8,128)(2,1)S(1)}, bf16[24,3584]{1,0:T(8,128)(2,1)S(1)}, u32[]{:S(2)}, u32[]{:S(2)}) collective-permute-start(bf16[24,3584]{1,0:T(8,128)(2,1)S(1)} %get-tuple-element.36), channel_id=1, source_target_pairs={{0,1},{1,2},{2,3},{3,0},{4,5},{5,6},{6,7},{7,4},{8,9},{9,10},{10,1... | collective-permute-start | bytes 516104 | tf_op jit(solution)/shard_map/ppermute | solution.py:385
